TPU v7x, 128 devices: a whole 4x4x4 slice. The times are simulated.
128 devices in a mesh: dp: 8 (over x, core), dap: 16 (over y, z).
Axes of the slice: x: 4, y: 4, z: 4, core: 2. Of those that a mesh axis runs over, the one named last changes fastest.
Arguments:
- pair_act: bfloat16 [8, 256, 256, 128], P('dp', 'dap'), may hold values from -6 to 6
- cotangent: bfloat16 [8, 256, 256, 128], P('dp', 'dap'), may hold values from -6 to 6
- residue_mask: int32 [8, 256], P('dp'), may hold values 0 or 1
- weights: bfloat16 [4, 128, 128], replicated, may hold values from -0.5 to 0.5
- error_in: float32 [8, 4, 128, 128], P('dp'), may hold values from -6 to 6
- q_init: float32 [4, 128, 32], replicated, may hold values from -6 to 6
Outputs:
- grad_pair: bfloat16 [8, 256, 256, 128], P('dp', 'dap')
- update: float32 [4, 128, 128], replicated
- error_out: float32 [8, 4, 128, 128], P('dp')
Inputs may be any that keep to these rules, and one draw needn't show every extreme that they name: `residue_mask`: 1 marks a present residue, 0 an absent one.
All inputs are finite; a program needn't handle non-finite values. No bound on the sum of `residue_mask` on one device may be relied on, other than what follows from the above.
Results may differ from a plain program's by a relative error of at most 0.02.
Values may be sent and summed in bfloat16 or wider, within the bound.
A program may use at most 192 MiB of HBM per device.

v0:
```python
import jax
import jax.numpy as jnp
from jax import lax
from jax.sharding import PartitionSpec as P

EPS = 1e-05
HIGH = lax.Precision.HIGHEST


def layer_norm(values):
    centre = values - jnp.mean(values, axis=-1, keepdims=True)
    inverse = lax.rsqrt(jnp.mean(centre * centre, axis=-1, keepdims=True) + EPS)
    return (centre * inverse, inverse)


def norm_back(upstream, normal, inverse):
    first = jnp.mean(upstream, axis=-1, keepdims=True)
    second = jnp.mean(upstream * normal, axis=-1, keepdims=True)
    return inverse * (upstream - first - normal * second)


def matmul(left_op, right_op):
    return jnp.dot(left_op, right_op, preferred_element_type=jnp.float32)


def flat_gram(left_op, right_op):
    width = left_op.shape[-1]
    return matmul(left_op.reshape(-1, width).T, right_op.reshape(-1, right_op.shape[-1]))


def orthonormal(panel):
    columns = []
    for column in range(panel.shape[1]):
        vector = panel[:, column]
        for basis_col in columns:
            vector = vector - jnp.dot(basis_col, vector, precision=HIGH) * basis_col
        columns.append(vector / jnp.sqrt(jnp.dot(vector, vector, precision=HIGH)))
    return jnp.stack(columns, axis=1)


def per_device(pair_act, cotangent, residue_mask, weights, error_in, q_init):
    pair_tile = pair_act[0]
    upstream = cotangent[0]
    rows, length, width = pair_tile.shape
    replicas = lax.axis_size("dp")
    w_left, w_right, w_gate, w_out = (weights[0], weights[1], weights[2], weights[3])
    keep = residue_mask[0].astype(jnp.float32)
    keep_rows = lax.dynamic_slice_in_dim(keep, lax.axis_index("dap") * rows, rows, 0)
    pair_mask = (keep_rows[:, None] * keep[None, :])[:, :, None]
    z_hat, z_inv = layer_norm(pair_tile.astype(jnp.float32))
    normed = z_hat.astype(jnp.bfloat16)
    left_act = (pair_mask * matmul(normed, w_left)).astype(jnp.bfloat16)
    right_act = (pair_mask * matmul(normed, w_right)).astype(jnp.bfloat16)
    piece = lax.all_gather(right_act, "dap", axis=0, tiled=True)
    product = jnp.einsum("ikc,jkc->ijc", left_act, piece, preferred_element_type=jnp.float32)
    x_hat, x_inv = layer_norm(product)
    x_normed = x_hat.astype(jnp.bfloat16)
    upstream_cols = upstream.astype(jnp.float32)
    gate = jax.nn.sigmoid(matmul(normed, w_gate))
    projected = matmul(x_normed, w_out)
    grad_proj = (upstream_cols * gate).astype(jnp.bfloat16)
    grad_logit = (upstream_cols * projected * gate * (1.0 - gate)).astype(jnp.bfloat16)
    grad_prod = norm_back(matmul(grad_proj, w_out.T), x_hat, x_inv).astype(jnp.bfloat16)
    grad_left = jnp.einsum("ijc,jkc->ikc", grad_prod, piece, preferred_element_type=jnp.float32)
    logit_store = grad_logit
    gate_grad = flat_gram(normed, grad_logit)
    out_grad = flat_gram(x_normed, grad_proj)
    grad_left, grad_store, logit_store, gate_grad, out_grad = (
        grad_left,
        grad_prod,
        logit_store,
        gate_grad,
        out_grad,
    )
    grad_right = lax.psum_scatter(
        jnp.einsum("ijc,ikc->jkc", grad_store, left_act, preferred_element_type=jnp.float32),
        "dap",
        scatter_dimension=0,
        tiled=True,
    )
    masked_left = (pair_mask * grad_left).astype(jnp.bfloat16)
    masked_right = (pair_mask * grad_right).astype(jnp.bfloat16)
    grad_normed = (
        matmul(logit_store, w_gate.T)
        + matmul(masked_left, w_left.T)
        + matmul(masked_right, w_right.T)
    )
    grad_pair = norm_back(grad_normed, z_hat, z_inv).astype(jnp.bfloat16)
    local_grads = jnp.stack(
        [flat_gram(normed, masked_left), flat_gram(normed, masked_right), gate_grad, out_grad]
    )
    crop_grads = lax.psum(local_grads.astype(jnp.bfloat16), "dap").astype(jnp.float32) / length
    memory = crop_grads + error_in[0]
    local_panel = jnp.einsum("wcd,wde->wce", memory, q_init, precision=HIGH)
    panel = lax.psum(local_panel, "dp") / replicas
    basis = jax.vmap(orthonormal)(panel)
    local_coeffs = jnp.einsum("wcd,wce->wde", memory, basis, precision=HIGH)
    coeffs = lax.psum(local_coeffs.astype(jnp.bfloat16), "dp").astype(jnp.float32) / replicas
    update = jnp.einsum("wce,wde->wcd", basis, coeffs, precision=HIGH)
    return (grad_pair[None], update, (memory - update)[None])


def solution(mesh):
    placed = (
        P("dp", "dap", None, None),
        P("dp", "dap", None, None),
        P("dp", None),
        P(),
        P("dp", None, None, None),
        P(),
    )
    return jax.shard_map(
        per_device,
        mesh=mesh,
        in_specs=placed,
        out_specs=(P("dp", "dap", None, None), P(), P("dp", None, None, None)),
        check_vma=False,
    )
```

profile of v0, /device:TPU:1, one launch (start us, length us, event | category | flops | bytes accessed | tf_op | source)
XLA Modules:
  0.0 627.0 jit_solution(5571965822689064025)
XLA Ops:
  7.9 1.5 copy.971
  10.1 1.8 multiply_convert_fusion.3
  12.0 1.0 multiply_convert_fusion.2
  13.0 1.7 copy.975
  14.7 0.8 add_divide_fusion
  16.4 0.9 copy-done.1
  17.2 109.5 %all-gather.2.cloned.1.call-done = bf16[256,256,128]{2,1,0:T(8,128)(2,1)} async-done(((bf16[16,256,128]{2,1,0:T(8,128)(2,1)}), bf16[256,256,128]{2,1,0:T(8,128)(2,1)}) %all-gather.2.cloned.1.call-update) | async-done | bytes 16777232 | tf_op jit(solution)/shard_map/all_gather | solution.py:54
  126.7 22.0 %copy.974 = bf16[256,256,128]{1,0,2:T(8,128)(2,1)} copy(bf16[256,256,128]{2,1,0:T(8,128)(2,1)} %all-gather.2.cloned.1.call-done) | data formatting | bytes 33554432 | tf_op jit(solution)/shard_map/all_gather | solution.py:54
  148.7 8.4 %bitcast_reduce_fusion = (f32[16,256]{1,0:T(8,128)S(1)}, f32[128,256,16]{1,2,0:T(8,128)S(1)}) fusion(bf16[256,256,128]{1,0,2:T(8,128)(2,1)} %copy.974, bf16[16,256,128]{1,0,2:T(8,128)(2,1)} %copy.975), kind=kOutput, calls=%fused_computation.25 | convolution fusion | flops 268955648 | bytes 19939328 | tf_op jit(solution)/shard_map/ikc,jkc->ijc/dot_general | solution.py:55
  157.4 1.5 multiply_reduce_fusion
  158.9 2.6 multiply_convert_fusion.1
  161.4 1.0 copy-done.5
  162.4 13.1 %fusion.103 = f32[128,256,256]{2,1,0:T(8,128)} fusion(bf16[16,256,128]{1,0,2:T(8,128)(2,1)S(1)} %copy-done.4, bf16[16,256,128]{1,0,2:T(8,128)(2,1)S(1)} %get-tuple-element.835), kind=kOutput, calls=%fused_computation.1246 | convolution fusion | flops 268435456 | bytes 35651584 | tf_op jit(solution)/shard_map/ijc,ikc->jkc/dot_general | solution.py:76
  175.5 31.5 %copy.983 = f32[128,256,256]{0,1,2:T(8,128)} copy(f32[128,256,256]{2,1,0:T(8,128)} %fusion.103) | data formatting | bytes 67108864 | tf_op jit(solution)/shard_map/ijc,ikc->jkc/dot_general | solution.py:76
  207.5 0.7 copy-done.6
  208.2 9.4 %fusion.104 = f32[128,256,16]{1,2,0:T(8,128)} fusion(bf16[16,256,128]{1,0,2:T(8,128)(2,1)S(1)} %copy-done.6, bf16[256,256,128]{1,0,2:T(8,128)(2,1)} %copy.974), kind=kOutput, calls=%fused_computation.1247 | convolution fusion | flops 268435456 | bytes 19922944 | tf_op jit(solution)/shard_map/ijc,jkc->ikc/dot_general | solution.py:64
  217.7 3.1 copy.981
  220.7 2.4 fusion.2
  223.1 1.1 fusion.25
  224.8 0.9 fusion.27
  226.4 1.4 fusion.24
  227.7 1.8 fusion.47
  229.5 2.2 fusion.39
  231.7 170.0 %reduce-scatter.2.cloned.1.call-done = f32[16,256,128]{2,1,0:T(8,128)} async-done(((f32[256,256,128]{2,1,0:T(8,128)}), f32[16,256,128]{2,1,0:T(8,128)}) %reduce-scatter.2.cloned.1.call-update) | async-done | bytes 2097168 | tf_op jit(solution)/shard_map/reduce_scatter | solution.py:75
  401.7 4.8 fusion.101
  407.1 0.9 fusion.26
  408.8 0.7 broadcast_multiply_fusion.2
  409.5 79.7 %all-reduce.3.cloned.1.call-done = bf16[4,128,128]{2,1,0:T(8,128)(2,1)} async-done(((bf16[4,128,128]{2,1,0:T(8,128)(2,1)}), bf16[4,128,128]{2,1,0:T(8,128)(2,1)}) %all-reduce.3.cloned.1.call-update) | async-done | bytes 131088 | tf_op jit(solution)/shard_map/psum | solution.py:92
  489.2 1.4 fusion.42
  490.7 0.7 copy.985
  491.4 2.3 fusion.29
  493.7 2.4 copy.990
  496.1 53.3 %all-reduce.5.cloned.1.call-done = f32[4,128,32]{1,0,2:T(4,128)} async-done(((f32[4,128,32]{1,0,2:T(4,128)}), f32[4,128,32]{1,0,2:T(4,128)}) %all-reduce.5.cloned.1.call-update) | async-done | bytes 65552 | tf_op jit(solution)/shard_map/psum | solution.py:95
  549.4 0.9 broadcast_multiply_fusion
  581.6 0.7 constant_dynamic-update-slice_fusion.11
  582.3 0.8 constant_dynamic-update-slice_fusion.10
  583.7 1.0 constant_dynamic-update-slice_fusion.9
  584.7 1.3 constant_dynamic-update-slice_fusion.8
  585.9 1.0 constant_dynamic-update-slice_fusion.7
  587.0 1.0 constant_dynamic-update-slice_fusion.6
  588.0 1.2 constant_dynamic-update-slice_fusion.5
  589.2 0.9 constant_dynamic-update-slice_fusion.4
  590.1 0.7 constant_dynamic-update-slice_fusion.3
  590.9 0.7 constant_dynamic-update-slice_fusion.2
  591.6 1.6 constant_dynamic-update-slice_fusion.1
  593.2 1.7 constant_dynamic-update-slice_fusion
  595.3 23.3 %psum.23 = bf16[4,128,32]{1,0,2:T(4,128)(2,1)S(1)} all-reduce(bf16[4,128,32]{1,0,2:T(4,128)(2,1)S(1)} %copy.3087), channel_id=1, replica_groups=mesh['dp'=8,'dap'=16] {'dp'}, use_global_device_ids=true, to_apply=%region_11.0 | all-reduce | flops 16384 | bytes 65536 | tf_op jit(solution)/shard_map/psum | solution.py:98
  619.3 0.8 subtract_bitcast_fusion
  (207 shorter events, 38.4 us)
Async XLA Ops:
  7.2 482.1 %copy-start = (f32[4,128,32]{1,2,0:T(8,128)S(1)}, f32[4,128,32]{1,2,0:T(8,128)}, u32[]{:S(2)}) copy-start(f32[4,128,32]{1,2,0:T(8,128)} %param.11) | copy-start | bytes 196612
  7.2 119.5 %all-gather.2.cloned.1.call-start = ((), (), s32[]{:S(2)}) async-start(), calls=%async_computation.1 | async-start | bytes 17825792 | tf_op jit(solution)/shard_map/all_gather | solution.py:54
  7.9 2.2 copy-start.14
  11.9 389.8 %reduce-scatter.2.cloned.1.call-start = ((), (), s32[]{:S(2)}) async-start(), calls=%async_computation.2 | async-start | bytes 35651584 | tf_op jit(solution)/shard_map/reduce_scatter | solution.py:75
  14.7 1.2 copy-start.7
  15.9 1.3 copy-start.1
  158.8 3.6 copy-start.4
  161.4 1.0 copy-start.5
  207.0 1.2 copy-start.6
  207.0 282.2 %all-reduce.3.cloned.1.call-start = ((), (), s32[]{:S(2)}) async-start(), calls=%async_computation.3 | async-start | bytes 262144 | tf_op jit(solution)/shard_map/psum | solution.py:92
  217.6 3.1 copy-start.2
  223.1 1.7 copy-start.3
  224.8 1.3 copy-start.8
  224.8 1.6 copy-start.9
  401.7 5.4 copy-start.10
  406.5 1.5 copy-start.15
  406.5 1.5 copy-start.16
  406.5 82.7 %copy-start.11 = (f32[1,4,128,128]{3,2,1,0:T(8,128)S(1)}, f32[1,4,128,128]{3,2,1,0:T(8,128)}, u32[]{:S(2)}) copy-start(f32[1,4,128,128]{3,2,1,0:T(8,128)} %param.10) | copy-start | bytes 786436
  408.7 140.7 %all-reduce.5.cloned.1.call-start = ((), (), s32[]{:S(2)}) async-start(), calls=%async_computation.4 | async-start | bytes 131072 | tf_op jit(solution)/shard_map/psum | solution.py:95
  571.8 23.1 %copy-start.12 = (bf16[4,128,128]{2,1,0:T(8,128)(2,1)S(1)}, bf16[4,128,128]{2,1,0:T(8,128)(2,1)}, u32[]{:S(2)}) copy-start(bf16[4,128,128]{2,1,0:T(8,128)(2,1)} %all-reduce.3.cloned.1.call-done) | copy-start | bytes 393220
  619.2 0.8 copy-start.13
Sparse Core Ops, SparseCore 0:
  12.0 114.6 all-gather.1
  207.1 194.5 reduce-scatter.1
  408.8 80.3 all-reduce.2
  492.1 57.2 all-reduce.4
where the time goes:
time: 638 us; the launch traced here: 627 us
  waiting for transfers between devices  413 us (65%)
  local copies, waits for them, and re-layouts  67.6 us (11%)
  other arithmetic  55.4 us (9%)
  matrix products  52.6 us (8%)
  blocking collectives  23.3 us (4%)
  between operations  14.7 us (2%)
    reduce_scatter x1, waiting for transfers between devices, per_device(): lax.psum_scatter(jnp.einsum('ijc,ikc->jkc', grad_store, left_act, preferr...  170 us
    all_gather x1, waiting for transfers between devices, per_device(): piece = lax.all_gather(right_act, 'dap', axis=0, tiled=True)  109 us
    psum x1, waiting for transfers between devices, per_device(): lax.psum(local_grads.astype(jnp.bfloat16), 'dap').astype(jnp.float32)  79.7 us
    psum x1, waiting for transfers between devices, per_device(): panel = lax.psum(local_panel, 'dp') / replicas  53.3 us
    dot_general x1, local copies, waits for them, and re-layouts, per_device(): jnp.einsum('ijc,ikc->jkc', grad_store, left_act, preferred_element_type=j...  31.5 us
    psum x1, blocking collectives, per_device(): lax.psum(local_coeffs.astype(jnp.bfloat16), 'dp').astype(jnp.float32)  23.3 us
    dot_general x74, other arithmetic, orthonormal(): vector = vector - jnp.dot(basis_col, vector, precision=HIGH) * basis_col  22.2 us
    all_gather x1, local copies, waits for them, and re-layouts, per_device(): piece = lax.all_gather(right_act, 'dap', axis=0, tiled=True)  22 us
  transfers between devices with their start and end apart: 4, of which 4 were waited for; matrix products, arithmetic and copies ran while one was open for 5% of the time, Pallas kernels for 0%

commit v1 on v0

v1 whole, which is shorter than its diff:
```python
import functools

import jax
import jax.numpy as jnp
from jax import lax
from jax.experimental import pallas as pl
from jax.experimental.pallas import tpu as pltpu
from jax.sharding import PartitionSpec as P

EPS = 1e-05
HIGH = lax.Precision.HIGHEST
MESH = pl.DeviceIdType.MESH
F32 = jnp.float32
BF16 = jnp.bfloat16
C = 128
N = 256
ROWS = 16
SLICE = 8
PITCH = 17
RANK = 32
DAP = 16
DP = 8
OFFSETS = sorted(
    [(dy, dz) for dy in range(4) for dz in range(4) if (dy, dz) != (0, 0)],
    key=lambda o: min(o[0], 4 - o[0]) + min(o[1], 4 - o[1]),
)


def nn(a, b):
    return lax.dot_general(a, b, (((1,), (0,)), ((), ())), preferred_element_type=F32)


def nt(a, b):
    return lax.dot_general(a, b, (((1,), (1,)), ((), ())), preferred_element_type=F32)


def tn(a, b):
    return lax.dot_general(a, b, (((0,), (0,)), ((), ())), preferred_element_type=F32)


def peers():
    me = lax.axis_index("dap")
    y, z = me // 4, lax.rem(me, 4)
    sign = 1 - 2 * lax.rem(lax.axis_index("dp"), 2)
    return [
        lax.rem(y + sign * dy + 4, 4) * 4 + lax.rem(z + sign * dz + 4, 4)
        for dy, dz in OFFSETS
    ]


def dap_barrier():
    me = lax.axis_index("dap")
    barrier = pltpu.get_barrier_semaphore()
    for step in range(1, DAP):
        pl.semaphore_signal(
            barrier, inc=1, device_id={"dap": lax.rem(me + step, DAP)}, device_id_type=MESH
        )
    pl.semaphore_wait(barrier, DAP - 1)


def to_channels(src, dst, half, send, recv, own):
    me = lax.axis_index("dap")
    lanes = pl.ds(half * 128, 128)
    rows = pl.ds(pl.multiple_of(me * ROWS, ROWS), ROWS)
    copies = []
    for t, peer in enumerate(peers()):
        copy = pltpu.make_async_remote_copy(
            src_ref=src.at[pl.ds(peer * SLICE, SLICE), :, lanes],
            dst_ref=dst.at[:, rows, lanes],
            send_sem=send.at[half, t],
            recv_sem=recv.at[half, t],
            device_id={"dap": peer},
            device_id_type=MESH,
        )
        copy.start()
        copies.append(copy)
    local = pltpu.make_async_copy(
        src.at[pl.ds(me * SLICE, SLICE), :, lanes], dst.at[:, rows, lanes], own.at[half]
    )
    local.start()
    return copies, local


def to_rows(src, dst, half, send, recv, own):
    me = lax.axis_index("dap")
    lanes = pl.ds(half * 128, 128)
    channels = pl.ds(me * SLICE, SLICE)
    copies = []
    for t, peer in enumerate(peers()):
        copy = pltpu.make_async_remote_copy(
            src_ref=src.at[:, pl.ds(pl.multiple_of(peer * ROWS, ROWS), ROWS), lanes],
            dst_ref=dst.at[channels, :, lanes],
            send_sem=send.at[half, t],
            recv_sem=recv.at[half, t],
            device_id={"dap": peer},
            device_id_type=MESH,
        )
        copy.start()
        copies.append(copy)
    local = pltpu.make_async_copy(
        src.at[:, pl.ds(pl.multiple_of(me * ROWS, ROWS), ROWS), lanes],
        dst.at[channels, :, lanes],
        own.at[half],
    )
    local.start()
    return copies, local


def arrive(started):
    copies, local = started
    for copy in copies:
        copy.wait_recv()
    local.wait()


def sent(started):
    for copy in started[0]:
        copy.wait_send()


def set_up(residue, weights, mask, lr_t, lr):
    me = lax.axis_index("dap")
    keep = residue[...].astype(F32)
    col = lax.broadcasted_iota(jnp.int32, (ROWS, N), 1)
    row = lax.broadcasted_iota(jnp.int32, (ROWS, N), 0) + me * ROWS
    keep_rows = jnp.sum(jnp.where(col == row, keep, 0.0), axis=1, keepdims=True)
    mask[...] = keep_rows * keep
    for w in range(2):
        lr_t[w * C : (w + 1) * C, :] = weights[w].astype(F32).T.astype(BF16)
        lr[:, w * C : (w + 1) * C] = weights[w]


def front(pair, lr_t, normed, z_hat, z_inv, tall):
    def step(i, _):
        x = pair[i].astype(F32)
        centre = x - jnp.sum(x, axis=-1, keepdims=True) * (1.0 / C)
        inv = lax.rsqrt(jnp.sum(centre * centre, axis=-1, keepdims=True) * (1.0 / C) + EPS)
        z = centre * inv
        nb = z.astype(BF16)
        normed[i] = nb
        z_hat[i] = z
        z_inv[i] = jnp.broadcast_to(inv, (N, C))
        both = nt(lr_t[...], nb)
        for w in range(2):
            for half in range(2):
                tall.at[w, half][pl.ds(i, C, stride=PITCH), :] = both[
                    w * C : (w + 1) * C, half * 128 : (half + 1) * 128
                ]
        return 0

    lax.fori_loop(0, ROWS, step, 0, unroll=2)


def pack(tall, w, half, mask, dst):
    m = mask[:, half * 128 : (half + 1) * 128]

    def step(b, _):
        for u in range(8):
            tile = tall[w, half, pl.ds(b * 8 * PITCH + u * PITCH, ROWS), :]
            dst[b * 8 + u, :, half * 128 : (half + 1) * 128] = (tile * m).astype(BF16)
        return 0

    lax.fori_loop(0, C // 8, step, 0)


def first_triangle(left, right, prod):
    def step(c, _):
        prod[c] = nt(left[c], right[c]).astype(BF16)
        return 0

    lax.fori_loop(0, SLICE, step, 0, unroll=2)


def mid_norm(x, half, tall, x_inv):
    lanes = slice(half * 128, (half + 1) * 128)

    def total(b, acc):
        for u in range(8):
            acc = acc + x[b * 8 + u, :, lanes].astype(F32)
        return acc

    mean = lax.fori_loop(0, C // 8, total, jnp.zeros((ROWS, 128), F32)) * (1.0 / C)

    def square(b, acc):
        for u in range(8):
            d = x[b * 8 + u, :, lanes].astype(F32) - mean
            acc = acc + d * d
        return acc

    var = lax.fori_loop(0, C // 8, square, jnp.zeros((ROWS, 128), F32)) * (1.0 / C)
    inv = lax.rsqrt(var + EPS)
    x_inv[:, lanes] = inv

    def store(b, _):
        for u in range(8):
            v = (x[b * 8 + u, :, lanes].astype(F32) - mean) * inv
            tall[0, half, pl.ds(b * 8 * PITCH + u * PITCH, ROWS), :] = v
        return 0

    lax.fori_loop(0, C // 8, store, 0)


def mid_mix(half, cot, normed, weights, tall, from_gate, grads):
    lanes = slice(half * 128, (half + 1) * 128)

    def step(i, carry):
        gate_grad, out_grad = carry
        xn = tall.at[0, half][pl.ds(i, C, stride=PITCH), :].astype(BF16)
        nb = normed[i, lanes, :]
        gate = jax.nn.sigmoid(nn(nb, weights[2]))
        projected = tn(xn, weights[3])
        up = cot[i, lanes, :].astype(F32)
        grad_proj = (up * gate).astype(BF16)
        grad_logit = (up * projected * gate * (1.0 - gate)).astype(BF16)
        gate_grad = gate_grad + tn(nb, grad_logit)
        out_grad = out_grad + nn(xn, grad_proj)
        tall.at[1, half][pl.ds(i, C, stride=PITCH), :] = nt(weights[3], grad_proj)
        from_gate[i, lanes, :] = nt(grad_logit, weights[2])
        return gate_grad, out_grad

    zero = jnp.zeros((C, C), F32)
    gate_grad, out_grad = lax.fori_loop(0, ROWS, step, (zero, zero), unroll=2)
    if half == 0:
        grads[2] = gate_grad
        grads[3] = out_grad
    else:
        grads[2] = grads[2] + gate_grad
        grads[3] = grads[3] + out_grad


def mid_back(half, tall, x_inv, dst):
    lanes = slice(half * 128, (half + 1) * 128)

    def total(b, acc):
        first, second = acc
        for u in range(8):
            at = pl.ds(b * 8 * PITCH + u * PITCH, ROWS)
            h = tall[1, half, at, :]
            first = first + h
            second = second + h * tall[0, half, at, :]
        return first, second

    zero = jnp.zeros((ROWS, 128), F32)
    first, second = lax.fori_loop(0, C // 8, total, (zero, zero))
    first = first * (1.0 / C)
    second = second * (1.0 / C)
    inv = x_inv[:, lanes]

    def store(b, _):
        for u in range(8):
            at = pl.ds(b * 8 * PITCH + u * PITCH, ROWS)
            v = inv * (tall[1, half, at, :] - first - tall[0, half, at, :] * second)
            dst[b * 8 + u, :, lanes] = v.astype(BF16)
        return 0

    lax.fori_loop(0, C // 8, store, 0)


def second_triangle(grad, left, right, to_left, to_right):
    def step(c, _):
        g = grad[c]
        to_left[c] = nn(g, right[c]).astype(BF16)
        to_right[c] = tn(g, left[c]).astype(BF16)
        return 0

    lax.fori_loop(0, SLICE, step, 0, unroll=2)


def unpack(src, w, half, mask, tall):
    lanes = slice(half * 128, (half + 1) * 128)
    m = mask[:, lanes]

    def step(b, _):
        for u in range(8):
            tall[w, half, pl.ds(b * 8 * PITCH + u * PITCH, ROWS), :] = (
                src[b * 8 + u, :, lanes].astype(F32) * m
            )
        return 0

    lax.fori_loop(0, C // 8, step, 0)


def last(half, tall, normed, z_hat, z_inv, from_gate, lr, out, grads):
    lanes = slice(half * 128, (half + 1) * 128)

    def step(i, acc):
        parts = [tall.at[w, half][pl.ds(i, C, stride=PITCH), :].astype(BF16) for w in range(2)]
        both = jnp.concatenate(parts, axis=0)
        acc = acc + nn(both, normed[i, lanes, :])
        grad = nn(lr[...], both).T + from_gate[i, lanes, :]
        z = z_hat[i, lanes, :]
        first = jnp.sum(grad, axis=-1, keepdims=True) * (1.0 / C)
        second = jnp.sum(grad * z, axis=-1, keepdims=True) * (1.0 / C)
        out[i, lanes, :] = (z_inv[i, lanes, :] * (grad - first - z * second)).astype(BF16)
        return acc

    acc = lax.fori_loop(0, ROWS, step, jnp.zeros((2 * C, C), F32), unroll=2)
    for w in range(2):
        if half == 0:
            grads[w] = acc[w * C : (w + 1) * C].T
        else:
            grads[w] = grads[w] + acc[w * C : (w + 1) * C].T


def main_kernel(
    pair, cot, residue, weights, out, grads,
    mask, lr_t, lr, normed, z_hat, z_inv, from_gate, x_inv, tall,
    send_l, send_r, left, right, prod, x, send_g, grad, to_l, to_r, got_l, got_r,
    send, recv, own,
):
    dap_barrier()
    set_up(residue, weights, mask, lr_t, lr)
    front(pair, lr_t, normed, z_hat, z_inv, tall)
    started = []
    for half in range(2):
        for w, (src, dst) in enumerate([(send_l, left), (send_r, right)]):
            pack(tall, w, half, mask, src)
            started.append(to_channels(src, dst, half, send.at[w], recv.at[w], own.at[w]))
    for s in started:
        arrive(s)
    first_triangle(left, right, prod)
    back = [to_rows(prod, x, half, send.at[2], recv.at[2], own.at[2]) for half in range(2)]
    again = []
    for half in range(2):
        arrive(back[half])
        mid_norm(x, half, tall, x_inv)
        mid_mix(half, cot, normed, weights, tall, from_gate, grads)
        mid_back(half, tall, x_inv, send_g)
        again.append(to_channels(send_g, grad, half, send.at[3], recv.at[3], own.at[3]))
    for s in again:
        arrive(s)
    second_triangle(grad, left, right, to_l, to_r)
    ends = []
    for half in range(2):
        for w, (src, dst) in enumerate([(to_l, got_l), (to_r, got_r)]):
            ends.append(to_rows(src, dst, half, send.at[4 + w], recv.at[4 + w], own.at[4 + w]))
    for half in range(2):
        for w, src in enumerate([got_l, got_r]):
            arrive(ends[2 * half + w])
            unpack(src, w, half, mask, tall)
        last(half, tall, normed, z_hat, z_inv, from_gate, lr, out, grads)
    for s in started + back + again + ends:
        sent(s)


def main_call(pair, cot, residue, weights):
    vmem = pl.BlockSpec(memory_space=pltpu.VMEM)
    by_rows = pltpu.VMEM((C, ROWS, N), BF16)
    by_channels = pltpu.VMEM((SLICE, N, N), BF16)
    wide = pltpu.VMEM((ROWS, N, C), F32)
    return pl.pallas_call(
        main_kernel,
        name="triangle",
        out_shape=(
            jax.ShapeDtypeStruct((ROWS, N, C), BF16),
            jax.ShapeDtypeStruct((4, C, C), F32),
        ),
        in_specs=[vmem] * 4,
        out_specs=(vmem, vmem),
        scratch_shapes=[
            pltpu.VMEM((ROWS, N), F32),
            pltpu.VMEM((2 * C, C), BF16),
            pltpu.VMEM((C, 2 * C), BF16),
            pltpu.VMEM((ROWS, N, C), BF16),
            wide,
            wide,
            wide,
            pltpu.VMEM((ROWS, N), F32),
            pltpu.VMEM((2, 2, C * PITCH, 128), F32),
            by_rows, by_rows, by_channels, by_channels,
            by_channels, by_rows,
            by_rows, by_channels,
            by_channels, by_channels, by_rows, by_rows,
            pltpu.SemaphoreType.DMA((6, 2, DAP - 1)),
            pltpu.SemaphoreType.DMA((6, 2, DAP - 1)),
            pltpu.SemaphoreType.DMA((6, 2)),
        ],
        compiler_params=pltpu.CompilerParams(
            collective_id=0, has_side_effects=True, vmem_limit_bytes=56 << 20
        ),
    )(pair, cot, residue, weights)


def orthonormal(panel):
    columns = []
    for column in range(panel.shape[1]):
        vector = panel[:, column]
        for basis_col in columns:
            vector = vector - jnp.dot(basis_col, vector, precision=HIGH) * basis_col
        columns.append(vector / jnp.sqrt(jnp.dot(vector, vector, precision=HIGH)))
    return jnp.stack(columns, axis=1)


def per_device(pair_act, cotangent, residue_mask, weights, error_in, q_init):
    replicas = lax.axis_size("dp")
    grad_pair, local_grads = main_call(pair_act[0], cotangent[0], residue_mask, weights)
    crop_grads = lax.psum(local_grads.astype(BF16), "dap").astype(F32) / N
    memory = crop_grads + error_in[0]
    local_panel = jnp.einsum("wcd,wde->wce", memory, q_init, precision=HIGH)
    panel = lax.psum(local_panel, "dp") / replicas
    basis = jax.vmap(orthonormal)(panel)
    local_coeffs = jnp.einsum("wcd,wce->wde", memory, basis, precision=HIGH)
    coeffs = lax.psum(local_coeffs.astype(jnp.bfloat16), "dp").astype(jnp.float32) / replicas
    update = jnp.einsum("wce,wde->wcd", basis, coeffs, precision=HIGH)
    return (grad_pair[None], update, (memory - update)[None])


def solution(mesh):
    placed = (
        P("dp", "dap", None, None),
        P("dp", "dap", None, None),
        P("dp", None),
        P(),
        P("dp", None, None, None),
        P(),
    )
    return jax.shard_map(
        per_device,
        mesh=mesh,
        in_specs=placed,
        out_specs=(P("dp", "dap", None, None), P(), P("dp", None, None, None)),
        check_vma=False,
    )
```

time: 638 us -> 331 us (0.52); the launches traced: 627 us -> 329 us
  waiting for transfers between devices: 413 us -> 140 us
  Pallas kernels: 0 us -> 98.8 us
  local copies, waits for them, and re-layouts: 67.6 us -> 2 us
  matrix products: 52.6 us -> 2.39 us
  other arithmetic: 55.4 us -> 47.3 us
    reduce_scatter x1 -> x0, waiting for transfers between devices: 170 us -> none  [per_device(): lax.psum_scatter(jnp.einsum('ijc,ikc->jkc', grad_store, left_act, preferr...]
    all_gather x1 -> x0, waiting for transfers between devices: 109 us -> none  [per_device(): piece = lax.all_gather(right_act, 'dap', axis=0, tiled=True)]
    pallas_call x0 -> x1, Pallas kernels: none -> 98.8 us  [main_call(): pl.pallas_call(main_kernel, name='triangle', out_shape=(jax.ShapeDtypeStr...]
    dot_general x15 -> x0, matrix products: 50.2 us -> none  [the longest x12 19.3 us: matmul(): return jnp.dot(left_op, right_op, preferred_element_type=jnp.float32)]
    dot_general x2 -> x0, local copies, waits for them, and re-layouts: 34.6 us -> none  [the longest x1 31.5 us: per_device(): jnp.einsum('ijc,ikc->jkc', grad_store, left_act, preferred_element_type=j...]
    all_gather x1 -> x0, local copies, waits for them, and re-layouts: 22 us -> none  [per_device(): piece = lax.all_gather(right_act, 'dap', axis=0, tiled=True)]
    unnamed x43 -> x18, local copies, waits for them, and re-layouts: 8.3 us -> 1.06 us
  transfers between devices with their start and end apart: 4 -> 2, of which waited for: 4 -> 2; matrix products, arithmetic and copies ran while one was open for 5% -> 0% of each run, Pallas kernels for 0% -> 0%
where the time goes in v1:
time: 331 us; the launch traced here: 329 us
  waiting for transfers between devices  140 us (42%)
  Pallas kernels  98.8 us (30%)
  other arithmetic  47.3 us (14%)
  blocking collectives  23.3 us (7%)
  between operations  14.5 us (4%)
    pallas_call x1, Pallas kernels, main_call(): pl.pallas_call(main_kernel, name='triangle', out_shape=(jax.ShapeDtypeStr...  98.8 us
    psum x1, waiting for transfers between devices, per_device(): crop_grads = lax.psum(local_grads.astype(BF16), 'dap').astype(F32) / N  82.2 us
    psum x1, waiting for transfers between devices, per_device(): panel = lax.psum(local_panel, 'dp') / replicas  58.2 us
    psum x1, blocking collectives, per_device(): lax.psum(local_coeffs.astype(jnp.bfloat16), 'dp').astype(jnp.float32)  23.3 us
    dot_general x74, other arithmetic, orthonormal(): vector = vector - jnp.dot(basis_col, vector, precision=HIGH) * basis_col  22.4 us
    unnamed x24, other arithmetic  15.1 us
  transfers between devices with their start and end apart: 2, of which 2 were waited for; matrix products, arithmetic and copies ran while one was open for 0% of the time, Pallas kernels for 0%

profile of v1, /device:TPU:1, one launch (start us, length us, event | category | flops | bytes accessed | tf_op | source)
XLA Modules:
  0.0 328.9 jit_solution(16079007846074203965)
XLA Ops:
  7.2 98.8 %triangle.1 = (bf16[16,256,128]{2,1,0:T(8,128)(2,1)}, f32[4,128,128]{2,1,0:T(8,128)}) custom-call(bf16[16,256,128]{2,1,0:T(8,128)(2,1)} %bitcast.208, bf16[16,256,128]{2,1,0:T(8,128)(2,1)} %bitcast.209, s32[1,256]{1,0:T(1,128)} %residue.1, bf16[4,128,128]{2,1,0:T(8,128)(2,1)} %weights.1), custom_call_target="tpu_custom_call" | custom-call | tf_op jit(solution)/shard_map/triangle/pallas_call | solution.py:351
  106.0 1.7 convert_element_type.12
  107.9 82.2 %all-reduce.3.cloned.1.call-done = bf16[4,128,128]{2,1,0:T(8,128)(2,1)} async-done(((bf16[4,128,128]{2,1,0:T(8,128)(2,1)}), bf16[4,128,128]{2,1,0:T(8,128)(2,1)}) %all-reduce.3.cloned.1.call-update) | async-done | bytes 131088 | tf_op jit(solution)/shard_map/psum | solution.py:397
  190.1 1.4 fusion.1
  191.5 0.7 copy.475
  192.3 58.2 %all-reduce.5.cloned.1.call-done = f32[4,128,32]{1,0,2:T(4,128)} async-done(((f32[4,128,32]{1,0,2:T(4,128)}), f32[4,128,32]{1,0,2:T(4,128)}) %all-reduce.5.cloned.1.call-update) | async-done | bytes 65552 | tf_op jit(solution)/shard_map/psum | solution.py:400
  250.4 0.9 broadcast_multiply_fusion
  251.4 0.5 fusion.6
  252.4 0.5 multiply_reduce_fusion.30
  254.9 0.5 multiply_reduce_fusion.28
  257.4 0.5 multiply_reduce_fusion.26
  259.8 0.5 multiply_reduce_fusion.24
  262.0 0.5 multiply_reduce_fusion.22
  264.1 0.5 multiply_reduce_fusion.20
  265.0 0.4 multiply_reduce_fusion.19
  266.5 0.5 multiply_reduce_fusion.18
  268.0 0.5 multiply_reduce_fusion.16
  269.5 0.4 multiply_reduce_fusion.15
  270.6 0.4 multiply_reduce_fusion.14
  271.0 0.4 multiply_reduce_fusion.13
  272.1 0.4 multiply_reduce_fusion.12
  272.5 0.4 multiply_reduce_fusion.11
  273.4 0.4 multiply_reduce_fusion.10
  273.8 0.4 multiply_reduce_fusion.9
  276.7 0.4 multiply_reduce_fusion.4
  280.1 0.4 constant_dynamic-update-slice_fusion.16
  280.5 0.5 constant_dynamic-update-slice_fusion.15
  280.9 0.5 constant_dynamic-update-slice_fusion.14
  281.4 0.6 constant_dynamic-update-slice_fusion.13
  282.0 0.6 constant_dynamic-update-slice_fusion.12
  282.7 0.7 constant_dynamic-update-slice_fusion.11
  283.4 0.8 constant_dynamic-update-slice_fusion.10
  284.2 0.6 subtract_divide_fusion.6
  284.7 1.0 constant_dynamic-update-slice_fusion.9
  285.7 1.3 constant_dynamic-update-slice_fusion.8
  287.0 1.0 constant_dynamic-update-slice_fusion.7
  288.0 1.0 constant_dynamic-update-slice_fusion.6
  289.0 1.2 constant_dynamic-update-slice_fusion.5
  290.3 0.9 constant_dynamic-update-slice_fusion.4
  291.2 0.7 constant_dynamic-update-slice_fusion.3
  291.9 0.7 constant_dynamic-update-slice_fusion.2
  292.6 1.6 constant_dynamic-update-slice_fusion.1
  294.2 1.7 constant_dynamic-update-slice_fusion
  296.0 0.4 fusion
  296.3 23.3 %psum.23 = bf16[4,128,32]{1,0,2:T(4,128)(2,1)S(1)} all-reduce(bf16[4,128,32]{1,0,2:T(4,128)(2,1)S(1)} %copy.2566), channel_id=1, replica_groups=mesh['dp'=8,'dap'=16] {'dp'}, use_global_device_ids=true, to_apply=%region_2.0 | all-reduce | flops 16384 | bytes 65536 | tf_op jit(solution)/shard_map/psum | solution.py:403
  319.7 0.6 fusion.2
  320.3 0.8 subtract_bitcast_fusion
  321.1 1.0 copy.2601
  (142 shorter events, 20.9 us)
Async XLA Ops:
  7.2 182.9 %copy-start = (f32[4,128,32]{1,2,0:T(8,128)S(1)}, f32[4,128,32]{1,2,0:T(8,128)}, u32[]{:S(2)}) copy-start(f32[4,128,32]{1,2,0:T(8,128)} %param.11) | copy-start | bytes 196612
  7.2 182.9 %all-reduce.3.cloned.1.call-start = ((), (), s32[]{:S(2)}) async-start(), calls=%async_computation | async-start | bytes 262144 | tf_op jit(solution)/shard_map/psum | solution.py:397
  106.0 84.1 %copy-start.1 = (f32[1,4,128,128]{3,2,1,0:T(8,128)S(1)}, f32[1,4,128,128]{3,2,1,0:T(8,128)}, u32[]{:S(2)}) copy-start(f32[1,4,128,128]{3,2,1,0:T(8,128)} %param.10) | copy-start | bytes 786436
  107.7 142.7 %all-reduce.5.cloned.1.call-start = ((), (), s32[]{:S(2)}) async-start(), calls=%async_computation.1 | async-start | bytes 131072 | tf_op jit(solution)/shard_map/psum | solution.py:400
  294.2 1.7 copy-start.2
  295.9 25.2 %copy-start.4 = (bf16[16,256,128]{2,1,0:T(8,128)(2,1)S(1)}, bf16[16,256,128]{2,1,0:T(8,128)(2,1)}, u32[]{:S(2)}) copy-start(bf16[16,256,128]{2,1,0:T(8,128)(2,1)} %get-tuple-element.5) | copy-start | bytes 3145732
  320.3 0.8 copy-start.3
Sparse Core Ops, SparseCore 0:
  107.8 82.2 all-reduce.2
  193.1 57.2 all-reduce.4

commit v2 on v1

v2 whole, which is shorter than its diff:
```python
import functools

import jax
import jax.numpy as jnp
from jax import lax
from jax.experimental import pallas as pl
from jax.experimental.pallas import tpu as pltpu
from jax.sharding import PartitionSpec as P

EPS = 1e-05
HIGH = lax.Precision.HIGHEST
MESH = pl.DeviceIdType.MESH
F32 = jnp.float32
BF16 = jnp.bfloat16
C = 128
N = 256
ROWS = 16
SLICE = 8
PITCH = 17
RANK = 32
DAP = 16
DP = 8
OFFSETS = sorted(
    [(dy, dz) for dy in range(4) for dz in range(4) if (dy, dz) != (0, 0)],
    key=lambda o: min(o[0], 4 - o[0]) + min(o[1], 4 - o[1]),
)


def nn(a, b):
    return lax.dot_general(a, b, (((1,), (0,)), ((), ())), preferred_element_type=F32)


def nt(a, b):
    return lax.dot_general(a, b, (((1,), (1,)), ((), ())), preferred_element_type=F32)


def tn(a, b):
    return lax.dot_general(a, b, (((0,), (0,)), ((), ())), preferred_element_type=F32)


def peers():
    me = lax.axis_index("dap")
    y, z = me // 4, lax.rem(me, 4)
    sign = 1 - 2 * lax.rem(lax.axis_index("dp"), 2)
    return [
        lax.rem(y + sign * dy + 4, 4) * 4 + lax.rem(z + sign * dz + 4, 4)
        for dy, dz in OFFSETS
    ]


def greet():
    barrier = pltpu.get_barrier_semaphore()
    for axis, size in (("dap", DAP), ("dp", DP)):
        me = lax.axis_index(axis)
        for step in range(1, size):
            pl.semaphore_signal(
                barrier, inc=1, device_id={axis: lax.rem(me + step, size)}, device_id_type=MESH
            )


def greeted():
    pl.semaphore_wait(pltpu.get_barrier_semaphore(), DAP + DP - 2)


def remote(src, dst, send, recv, axis, peer):
    copy = pltpu.make_async_remote_copy(
        src_ref=src, dst_ref=dst, send_sem=send, recv_sem=recv,
        device_id={axis: peer}, device_id_type=MESH,
    )
    copy.start()
    return copy


def exchange(src, dst, half, send, recv):
    me = lax.axis_index("dap")
    for peer in peers():
        remote(src.at[half, peer], dst.at[half, me], send.at[half], recv.at[half], "dap", peer)
    pltpu.make_async_copy(src.at[half, me], dst.at[half, me], recv.at[half]).start()


def await_bytes(ref, sem):
    pltpu.make_async_copy(ref, ref, sem).wait()


def set_up(residue, weights, mask, lr_t, lr):
    me = lax.axis_index("dap")
    keep = residue[...].astype(F32)
    col = lax.broadcasted_iota(jnp.int32, (ROWS, N), 1)
    row = lax.broadcasted_iota(jnp.int32, (ROWS, N), 0) + me * ROWS
    keep_rows = jnp.sum(jnp.where(col == row, keep, 0.0), axis=1, keepdims=True)
    mask[...] = keep_rows * keep
    for w in range(2):
        lr_t[w * C : (w + 1) * C, :] = weights[w].astype(F32).T.astype(BF16)
        lr[:, w * C : (w + 1) * C] = weights[w]


def front(half, pair, lr_t, normed, z_hat, z_inv, tall):
    lanes = slice(half * 128, (half + 1) * 128)

    def step(i, _):
        x = pair[i, lanes, :].astype(F32)
        centre = x - jnp.sum(x, axis=-1, keepdims=True) * (1.0 / C)
        inv = lax.rsqrt(jnp.sum(centre * centre, axis=-1, keepdims=True) * (1.0 / C) + EPS)
        z = centre * inv
        nb = z.astype(BF16)
        normed[i, lanes, :] = nb
        z_hat[i, lanes, :] = z
        z_inv[i, lanes, :] = jnp.broadcast_to(inv, (128, C))
        both = nt(lr_t[...], nb)
        for w in range(2):
            tall.at[w, half][pl.ds(i, C, stride=PITCH), :] = both[w * C : (w + 1) * C]
        return 0

    lax.fori_loop(0, ROWS, step, 0, unroll=4)


def tile_at(b, u):
    return pl.ds(b * SLICE * PITCH + u * PITCH, ROWS)


def pack(tall, w, half, mask, dst):
    m = mask[:, half * 128 : (half + 1) * 128]

    def step(b, _):
        for u in range(SLICE):
            dst[half, b, u] = (tall[w, half, tile_at(b, u), :] * m).astype(BF16)
        return 0

    lax.fori_loop(0, DAP, step, 0)


def plane(ref, half, c):
    return ref[half, :, c].reshape(N, 128)


def whole(ref, c):
    return jnp.concatenate([plane(ref, 0, c), plane(ref, 1, c)], axis=1)


def first_triangle(half, left, right, prod):
    def step(c, _):
        cols = right[:, half * DAP // 2 : (half + 1) * DAP // 2, c]
        cols = jnp.concatenate([cols[0].reshape(128, 128), cols[1].reshape(128, 128)], axis=1)
        prod[half, :, c] = nt(whole(left, c), cols).astype(BF16).reshape(DAP, ROWS, 128)
        return 0

    lax.fori_loop(0, SLICE, step, 0, unroll=4)


def mid_norm(x, half, tall, x_inv):
    lanes = slice(half * 128, (half + 1) * 128)
    zero = jnp.zeros((ROWS, 128), F32)

    def total(b, acc):
        for u in range(SLICE):
            acc = acc + x[half, b, u].astype(F32)
        return acc

    mean = lax.fori_loop(0, DAP, total, zero) * (1.0 / C)

    def square(b, acc):
        for u in range(SLICE):
            d = x[half, b, u].astype(F32) - mean
            acc = acc + d * d
        return acc

    var = lax.fori_loop(0, DAP, square, zero) * (1.0 / C)
    inv = lax.rsqrt(var + EPS)
    x_inv[:, lanes] = inv

    def store(b, _):
        for u in range(SLICE):
            tall[0, half, tile_at(b, u), :] = (x[half, b, u].astype(F32) - mean) * inv
        return 0

    lax.fori_loop(0, DAP, store, 0)


def mid_mix(half, cot, normed, weights, tall, from_gate, grads):
    lanes = slice(half * 128, (half + 1) * 128)

    def step(i, carry):
        gate_grad, out_grad = carry
        xn = tall.at[0, half][pl.ds(i, C, stride=PITCH), :].astype(BF16)
        nb = normed[i, lanes, :]
        gate = jax.nn.sigmoid(nn(nb, weights[2]))
        projected = tn(xn, weights[3])
        up = cot[i, lanes, :].astype(F32)
        grad_proj = (up * gate).astype(BF16)
        grad_logit = (up * projected * gate * (1.0 - gate)).astype(BF16)
        gate_grad = gate_grad + tn(nb, grad_logit)
        out_grad = out_grad + nn(xn, grad_proj)
        tall.at[1, half][pl.ds(i, C, stride=PITCH), :] = nt(weights[3], grad_proj)
        from_gate[i, lanes, :] = nt(grad_logit, weights[2])
        return gate_grad, out_grad

    zero = jnp.zeros((C, C), F32)
    gate_grad, out_grad = lax.fori_loop(0, ROWS, step, (zero, zero), unroll=2)
    if half == 0:
        grads[2] = gate_grad
        grads[3] = out_grad
    else:
        grads[2] = grads[2] + gate_grad
        grads[3] = grads[3] + out_grad


def mid_back(half, tall, x_inv, dst):
    lanes = slice(half * 128, (half + 1) * 128)

    def total(b, acc):
        first, second = acc
        for u in range(SLICE):
            h = tall[1, half, tile_at(b, u), :]
            first = first + h
            second = second + h * tall[0, half, tile_at(b, u), :]
        return first, second

    zero = jnp.zeros((ROWS, 128), F32)
    first, second = lax.fori_loop(0, DAP, total, (zero, zero))
    first = first * (1.0 / C)
    second = second * (1.0 / C)
    inv = x_inv[:, lanes]

    def store(b, _):
        for u in range(SLICE):
            at = tile_at(b, u)
            v = inv * (tall[1, half, at, :] - first - tall[0, half, at, :] * second)
            dst[half, b, u] = v.astype(BF16)
        return 0

    lax.fori_loop(0, DAP, store, 0)


def grad_of_left(half, grad, right, dst):
    def step(c, _):
        dst[half, :, c] = nn(whole(grad, c), plane(right, half, c)).astype(BF16).reshape(DAP, ROWS, 128)
        return 0

    lax.fori_loop(0, SLICE, step, 0, unroll=4)


def grad_of_right(half, grad, left, dst):
    def step(c, _):
        dst[half, :, c] = tn(whole(grad, c), plane(left, half, c)).astype(BF16).reshape(DAP, ROWS, 128)
        return 0

    lax.fori_loop(0, SLICE, step, 0, unroll=4)


def unpack(src, w, half, mask, tall):
    m = mask[:, half * 128 : (half + 1) * 128]

    def step(b, _):
        for u in range(SLICE):
            tall[w, half, tile_at(b, u), :] = src[half, b, u].astype(F32) * m
        return 0

    lax.fori_loop(0, DAP, step, 0)


def both_sides(half, i, tall):
    return jnp.concatenate(
        [tall.at[w, half][pl.ds(i, C, stride=PITCH), :].astype(BF16) for w in range(2)], axis=0
    )


def last_grads(half, tall, normed, both, grads):
    lanes = slice(half * 128, (half + 1) * 128)

    def step(i, acc):
        pair = both_sides(half, i, tall)
        both[i] = pair
        return acc + nn(pair, normed[i, lanes, :])

    acc = lax.fori_loop(0, ROWS, step, jnp.zeros((2 * C, C), F32), unroll=4)
    for w in range(2):
        new = acc[w * C : (w + 1) * C].T
        grads[w] = new if half == 0 else grads[w] + new


def last_pair(half, both, z_hat, z_inv, from_gate, lr, out):
    lanes = slice(half * 128, (half + 1) * 128)

    def step(i, _):
        grad = nn(lr[...], both[i]).T + from_gate[i, lanes, :]
        z = z_hat[i, lanes, :]
        first = jnp.sum(grad, axis=-1, keepdims=True) * (1.0 / C)
        second = jnp.sum(grad * z, axis=-1, keepdims=True) * (1.0 / C)
        out[i, lanes, :] = (z_inv[i, lanes, :] * (grad - first - z * second)).astype(BF16)
        return 0

    lax.fori_loop(0, ROWS, step, 0, unroll=4)


def gram_schmidt(panel):
    row = lax.broadcasted_iota(jnp.int32, (8, 1), 0)
    for j in range(RANK):
        at, sub = j // 8, j % 8
        for tiles in panel:
            v = jnp.broadcast_to(tiles[at][sub : sub + 1, :], (8, C))
            dots = [
                jnp.sum(tiles[t] * v, axis=1, keepdims=True) if t >= at else None
                for t in range(RANK // 8)
            ]
            scale = 1.0 / jnp.broadcast_to(dots[at][sub : sub + 1, :], (8, 1))
            for t in range(at, RANK // 8):
                coef = dots[t] * scale
                if t == at:
                    coef = jnp.where(row > sub, coef, 0.0)
                tiles[t] = tiles[t] - coef * v
    return [
        jnp.concatenate(
            [t * lax.rsqrt(jnp.sum(t * t, axis=1, keepdims=True)) for t in tiles], axis=0
        )
        for tiles in panel
    ]


def compress(grads, error_in, q_init, update, error_out, bufs, sems, meanwhile):
    part16, got16, crop16, chunk, got32, mean = bufs
    send, recv = sems
    me, dp = lax.axis_index("dap"), lax.axis_index("dp")
    rows = 4 * C // DAP
    mine = pl.ds(pl.multiple_of(me * rows, rows), rows)
    others = peers()

    for w in range(4):
        part16[w * C : (w + 1) * C, :] = grads[w].astype(BF16)
    for t, peer in enumerate(others):
        block = part16.at[pl.ds(pl.multiple_of(peer * rows, rows), rows)]
        remote(block, got16.at[t], send.at[0], recv.at[0], "dap", peer)
    meanwhile()
    await_bytes(got16, recv.at[0])
    total = part16[mine, :].astype(F32)
    for t in range(DAP - 1):
        total = total + got16[t].astype(F32)
    crop16[mine, :] = (total * (1.0 / N)).astype(BF16)

    matrix, first = me // 4, pl.multiple_of(lax.rem(me, 4) * rows, rows)
    chunk[...] = crop16[mine, :].astype(F32) + error_in[matrix, pl.ds(first, rows), :]
    got32[dp] = chunk[...]
    for s in range(1, DP):
        remote(chunk, got32.at[dp], send.at[1], recv.at[1], "dp", lax.rem(dp + s, DP))
    for peer in others:
        remote(crop16.at[mine], crop16.at[mine], send.at[2], recv.at[2], "dap", peer)
    await_bytes(got32.at[pl.ds(0, DP - 1)], recv.at[1])
    total = got32[0]
    for r in range(1, DP):
        total = total + got32[r]
    mean[mine, :] = total * (1.0 / DP)
    for peer in others:
        remote(mean.at[mine], mean.at[mine], send.at[3], recv.at[3], "dap", peer)
    gathered = pl.ds(0, 4 * C - rows)
    await_bytes(mean.at[gathered], recv.at[3])

    panel = []
    for w in range(4):
        rows_of = lax.dot_general(
            q_init[w], mean[w * C : (w + 1) * C, :], (((1,), (1,)), ((), ())),
            preferred_element_type=F32, precision=HIGH,
        )
        panel.append([rows_of[t * 8 : (t + 1) * 8, :] for t in range(RANK // 8)])
    basis = gram_schmidt(panel)
    await_bytes(crop16.at[gathered], recv.at[2])
    for w in range(4):
        here = slice(w * C, (w + 1) * C)
        coeffs = lax.dot_general(
            basis[w], mean[here, :], (((1,), (0,)), ((), ())),
            preferred_element_type=F32, precision=HIGH,
        )
        new = lax.dot_general(
            basis[w], coeffs, (((0,), (0,)), ((), ())),
            preferred_element_type=F32, precision=HIGH,
        )
        update[w] = new
        error_out[w] = crop16[here, :].astype(F32) + error_in[w] - new
    await_bytes(part16.at[gathered], send.at[0])
    await_bytes(got32.at[pl.ds(0, DP - 1)], send.at[1])
    await_bytes(crop16.at[gathered], send.at[2])
    await_bytes(mean.at[gathered], send.at[3])


def main_kernel(
    pair_in, cot_in, error_at, q_at, residue, weights, out, update, error_out,
    pair, cot, error_in, q_init,
    grads, mask, lr_t, lr, normed, z_hat, z_inv, from_gate, x_inv, tall, both,
    send_l, send_r, left, right, prod, x, send_g, grad, to_l, to_r, got_l, got_r,
    part16, got16, crop16, chunk, got32, mean,
    fetch, send, recv, send_c, recv_c,
):
    fetched = []
    for k, (src, dst) in enumerate(
        [
            (pair_in.at[:, pl.ds(0, 128)], pair.at[:, pl.ds(0, 128)]),
            (pair_in.at[:, pl.ds(128, 128)], pair.at[:, pl.ds(128, 128)]),
            (cot_in, cot),
            (error_at, error_in),
            (q_at, q_init),
        ]
    ):
        copy = pltpu.make_async_copy(src, dst, fetch.at[k])
        copy.start()
        fetched.append(copy)
    greet()
    set_up(residue, weights, mask, lr_t, lr)
    started = []

    def begin(k, half, src, dst):
        exchange(src, dst, half, send.at[k], recv.at[k])
        started.append((src, half, k))

    def arrive(k, half, dst):
        await_bytes(dst.at[half], recv.at[k, half])

    sides = [(send_l, left), (send_r, right)]
    for half in range(2):
        fetched[half].wait()
        front(half, pair, lr_t, normed, z_hat, z_inv, tall)
        for w, (src, dst) in enumerate(sides):
            pack(tall, w, half, mask, src)
            if half == 0 and w == 0:
                greeted()
            begin(w, half, src, dst)
    for copy in fetched[2:]:
        copy.wait()
    for half in range(2):
        for w in range(2):
            arrive(w, half, sides[w][1])
    for half in range(2):
        first_triangle(half, left, right, prod)
        begin(2, half, prod, x)
    for half in range(2):
        arrive(2, half, x)
        mid_norm(x, half, tall, x_inv)
        mid_mix(half, cot, normed, weights, tall, from_gate, grads)
        mid_back(half, tall, x_inv, send_g)
        begin(3, half, send_g, grad)
    for half in range(2):
        arrive(3, half, grad)
    for half in range(2):
        grad_of_left(half, grad, right, to_l)
        begin(4, half, to_l, got_l)
        grad_of_right(half, grad, left, to_r)
        begin(5, half, to_r, got_r)
    for half in range(2):
        for w, src in enumerate([got_l, got_r]):
            arrive(4 + w, half, src)
            unpack(src, w, half, mask, tall)
        last_grads(half, tall, normed, both, grads)
        if half == 0:
            last_pair(half, both, z_hat, z_inv, from_gate, lr, out)
    compress(
        grads, error_in, q_init, update, error_out,
        (part16, got16, crop16, chunk, got32, mean), (send_c, recv_c),
        lambda: last_pair(1, both, z_hat, z_inv, from_gate, lr, out),
    )
    for src, half, k in started:
        await_bytes(src.at[half, pl.ds(0, DAP - 1)], send.at[k, half])


def main_call(*operands):
    vmem = pl.BlockSpec(memory_space=pltpu.VMEM)
    hbm = pl.BlockSpec(memory_space=pl.ANY)
    blocks = pltpu.VMEM((2, DAP, SLICE, ROWS, 128), BF16)
    wide = pltpu.VMEM((ROWS, N, C), F32)
    half_wide = pltpu.VMEM((ROWS, N, C), BF16)
    part = 4 * C // DAP
    return pl.pallas_call(
        main_kernel,
        name="triangle",
        out_shape=(
            pltpu.VMEM((ROWS, N, C), BF16),
            pltpu.VMEM((4, C, C), F32),
            pltpu.VMEM((4, C, C), F32),
        ),
        in_specs=[hbm] * 4 + [vmem] * 2,
        out_specs=(vmem, vmem, vmem),
        scratch_shapes=[
            half_wide,
            half_wide,
            pltpu.VMEM((4, C, C), F32),
            pltpu.VMEM((4, RANK, C), F32),
            pltpu.VMEM((4, C, C), F32),
            pltpu.VMEM((ROWS, N), F32),
            pltpu.VMEM((2 * C, C), BF16),
            pltpu.VMEM((C, 2 * C), BF16),
            half_wide,
            wide,
            wide,
            wide,
            pltpu.VMEM((ROWS, N), F32),
            pltpu.VMEM((2, 2, C * PITCH, 128), F32),
            pltpu.VMEM((ROWS, 2 * C, 128), BF16),
        ]
        + [blocks] * 12
        + [
            pltpu.VMEM((4 * C, C), BF16),
            pltpu.VMEM((DAP - 1, part, C), BF16),
            pltpu.VMEM((4 * C, C), BF16),
            pltpu.VMEM((part, C), F32),
            pltpu.VMEM((DP, part, C), F32),
            pltpu.VMEM((4 * C, C), F32),
            pltpu.SemaphoreType.DMA((5,)),
            pltpu.SemaphoreType.DMA((6, 2)),
            pltpu.SemaphoreType.DMA((6, 2)),
            pltpu.SemaphoreType.DMA((4,)),
            pltpu.SemaphoreType.DMA((4,)),
        ],
        compiler_params=pltpu.CompilerParams(
            collective_id=0, has_side_effects=True, vmem_limit_bytes=56 << 20
        ),
    )(*operands)


def store_kernel(*refs):
    sources, targets, sems = refs[:3], refs[3:6], refs[6]
    copies = [
        pltpu.make_async_copy(src, dst, sems.at[k])
        for k, (src, dst) in enumerate(zip(sources, targets))
    ]
    for copy in copies:
        copy.start()
    for copy in copies:
        copy.wait()


def store(*arrays):
    vmem = pl.BlockSpec(memory_space=pltpu.VMEM)
    hbm = pl.BlockSpec(memory_space=pl.ANY)
    return pl.pallas_call(
        store_kernel,
        name="store",
        out_shape=tuple(jax.ShapeDtypeStruct(a.shape, a.dtype) for a in arrays),
        in_specs=[vmem] * 3,
        out_specs=(hbm,) * 3,
        scratch_shapes=[pltpu.SemaphoreType.DMA((3,))],
        compiler_params=pltpu.CompilerParams(vmem_limit_bytes=8 << 20),
    )(*arrays)


def per_device(pair_act, cotangent, residue_mask, weights, error_in, q_init):
    results = main_call(
        pair_act[0], cotangent[0], error_in[0], q_init.transpose(0, 2, 1), residue_mask, weights
    )
    grad_pair, update, error_out = store(*results)
    return (grad_pair[None], update, error_out[None])


def solution(mesh):
    placed = (
        P("dp", "dap", None, None),
        P("dp", "dap", None, None),
        P("dp", None),
        P(),
        P("dp", None, None, None),
        P(),
    )
    return jax.shard_map(
        per_device,
        mesh=mesh,
        in_specs=placed,
        out_specs=(P("dp", "dap", None, None), P(), P("dp", None, None, None)),
        check_vma=False,
    )
```

time: 331 us -> 114 us (0.34)
  waiting for transfers between devices: 140 us -> 0 us
  other arithmetic: 47.3 us -> 0 us
  blocking collectives: 23.3 us -> 0 us
  Pallas kernels: 98.8 us -> 113 us
  between operations: 14.5 us -> 0.64 us
    psum x2 -> x0, waiting for transfers between devices: 140 us -> none  [the longest x1 82.2 us: per_device(): crop_grads = lax.psum(local_grads.astype(BF16), 'dap').astype(F32) / N]
    dot_general x91 -> x0, other arithmetic: 25.5 us -> none  [the longest x74 22.4 us: orthonormal(): vector = vector - jnp.dot(basis_col, vector, precision=HIGH) * basis_col]
    psum x1 -> x0, blocking collectives: 23.3 us -> none  [per_device(): lax.psum(local_coeffs.astype(jnp.bfloat16), 'dp').astype(jnp.float32)]
    unnamed x24 -> x0, other arithmetic: 15.1 us -> none
    pallas_call x1 -> x2, Pallas kernels: 98.8 us -> 113 us  [the longest x1 112 us: main_call(): pl.pallas_call(main_kernel, name='triangle', out_shape=(pltpu.VMEM((ROWS,...]
  transfers between devices with their start and end apart: 2 -> 0, of which waited for: 2 -> 0; matrix products, arithmetic and copies ran while one was open for 0% -> 0% of each run, Pallas kernels for 0% -> 0%
where the time goes in v2:
time: 114 us
  Pallas kernels  113 us (99%)
    pallas_call x1, Pallas kernels, main_call(): pl.pallas_call(main_kernel, name='triangle', out_shape=(pltpu.VMEM((ROWS,...  112 us

profile of v2, /device:TPU:1, one launch (start us, length us, event | category | flops | bytes accessed | tf_op | source)
XLA Modules:
  0.0 113.6 jit_solution(16854286115838856239)
XLA Ops:
  0.6 111.8 %triangle.1 = (bf16[16,256,128]{2,1,0:T(8,128)(2,1)S(1)}, f32[4,128,128]{2,1,0:T(8,128)S(1)}, f32[4,128,128]{2,1,0:T(8,128)S(1)}) custom-call(bf16[16,256,128]{2,1,0:T(8,128)(2,1)} %bitcast.6, bf16[16,256,128]{2,1,0:T(8,128)(2,1)} %bitcast.7, f32[4,128,128]{2,1,0:T(8,128)} %bitcast.8, f32[4,32,128]{2,1,0:T(8,128)} %bitcast.9, s32[1,256]{1,0:T(1,128)} %residue.1, ...), custom_call_target="tpu_custom_call" | custom-call | tf_op jit(solution)/shard_map/triangle/pallas_call | solution.py:468
  112.4 1.2 %store.1 = (bf16[16,256,128]{2,1,0:T(8,128)(2,1)}, f32[4,128,128]{2,1,0:T(8,128)}, f32[4,128,128]{2,1,0:T(8,128)}) custom-call(bf16[16,256,128]{2,1,0:T(8,128)(2,1)S(1)} %get-tuple-element.9.refs_0_, f32[4,128,128]{2,1,0:T(8,128)S(1)} %get-tuple-element.10.refs_1_, f32[4,128,128]{2,1,0:T(8,128)S(1)} %get-tuple-element.11.refs_2_), custom_call_target="tpu_custom_call" | custom-call | tf_op jit(solution)/shard_map/store/pallas_call | solution.py:530

commit v3 on v2

--- a/solution.py
+++ b/solution.py
@@ -20,10 +20,7 @@
 RANK = 32
 DAP = 16
 DP = 8
-OFFSETS = sorted(
-    [(dy, dz) for dy in range(4) for dz in range(4) if (dy, dz) != (0, 0)],
-    key=lambda o: min(o[0], 4 - o[0]) + min(o[1], 4 - o[1]),
-)
+OFFSETS = [(2,2),(1,2),(3,2),(2,1),(2,3),(1,1),(3,3),(1,3),(3,1),(2,0),(0,2),(1,0),(3,0),(0,1),(0,3)]
 
 
 def nn(a, b):
@@ -82,7 +79,7 @@
     pltpu.make_async_copy(ref, ref, sem).wait()
 
 
-def set_up(residue, weights, mask, lr_t, lr):
+def set_up(residue, weights, mask, lr_t, lr, gate_t):
     me = lax.axis_index("dap")
     keep = residue[...].astype(F32)
     col = lax.broadcasted_iota(jnp.int32, (ROWS, N), 1)
@@ -92,9 +89,10 @@
     for w in range(2):
         lr_t[w * C : (w + 1) * C, :] = weights[w].astype(F32).T.astype(BF16)
         lr[:, w * C : (w + 1) * C] = weights[w]
-
-
-def front(half, pair, lr_t, normed, z_hat, z_inv, tall):
+    gate_t[...] = weights[2].astype(F32).T.astype(BF16)
+
+
+def front(half, pair, lr_t, normed, normed_t, z_hat, z_inv, tall):
     lanes = slice(half * 128, (half + 1) * 128)
 
     def step(i, _):
@@ -103,15 +101,39 @@
         inv = lax.rsqrt(jnp.sum(centre * centre, axis=-1, keepdims=True) * (1.0 / C) + EPS)
         z = centre * inv
         nb = z.astype(BF16)
+        nb_t = nb.T
         normed[i, lanes, :] = nb
+        normed_t[half, i] = nb_t
         z_hat[i, lanes, :] = z
         z_inv[i, lanes, :] = jnp.broadcast_to(inv, (128, C))
-        both = nt(lr_t[...], nb)
+        both = nn(lr_t[...], nb_t)
         for w in range(2):
             tall.at[w, half][pl.ds(i, C, stride=PITCH), :] = both[w * C : (w + 1) * C]
         return 0
 
     lax.fori_loop(0, ROWS, step, 0, unroll=4)
+
+
+def gating(half, cot, normed, weights, gate, grad_proj, tall, h_mean):
+    lanes = slice(half * 128, (half + 1) * 128)
+
+    def step(i, _):
+        g = jax.nn.sigmoid(nn(normed[i, lanes, :], weights[2]))
+        gp = (cot[i, lanes, :].astype(F32) * g).astype(BF16)
+        gate[i, lanes, :] = g
+        grad_proj[i, lanes, :] = gp
+        tall.at[1, half][pl.ds(i, C, stride=PITCH), :] = nt(weights[3], gp)
+        return 0
+
+    lax.fori_loop(0, ROWS, step, 0, unroll=4)
+
+    def total(b, acc):
+        for u in range(SLICE):
+            acc = acc + tall[1, half, tile_at(b, u), :]
+        return acc
+
+    zero = jnp.zeros((ROWS, 128), F32)
+    h_mean[:, lanes] = lax.fori_loop(0, DAP, total, zero) * (1.0 / C)
 
 
 def tile_at(b, u):
@@ -147,7 +169,7 @@
     lax.fori_loop(0, SLICE, step, 0, unroll=4)
 
 
-def mid_norm(x, half, tall, x_inv):
+def mid_core(half, x, tall, h_mean, x_mean, x_inv, dst):
     lanes = slice(half * 128, (half + 1) * 128)
     zero = jnp.zeros((ROWS, 128), F32)
 
@@ -159,76 +181,58 @@
     mean = lax.fori_loop(0, DAP, total, zero) * (1.0 / C)
 
     def square(b, acc):
+        squares, dots = acc
         for u in range(SLICE):
             d = x[half, b, u].astype(F32) - mean
-            acc = acc + d * d
-        return acc
-
-    var = lax.fori_loop(0, DAP, square, zero) * (1.0 / C)
-    inv = lax.rsqrt(var + EPS)
+            squares = squares + d * d
+            dots = dots + d * tall[1, half, tile_at(b, u), :]
+        return squares, dots
+
+    squares, dots = lax.fori_loop(0, DAP, square, (zero, zero))
+    inv = lax.rsqrt(squares * (1.0 / C) + EPS)
+    second = dots * inv * (1.0 / C)
+    first = h_mean[:, lanes]
+    x_mean[:, lanes] = mean
     x_inv[:, lanes] = inv
 
     def store(b, _):
         for u in range(SLICE):
+            x_hat = (x[half, b, u].astype(F32) - mean) * inv
+            v = inv * (tall[1, half, tile_at(b, u), :] - first - x_hat * second)
+            dst[half, b, u] = v.astype(BF16)
+        return 0
+
+    lax.fori_loop(0, DAP, store, 0)
+
+
+def mid_rest(half, x, x_mean, x_inv, cot, normed_t, gate, grad_proj, weights, gate_t, tall, from_gate, grads):
+    lanes = slice(half * 128, (half + 1) * 128)
+    mean = x_mean[:, lanes]
+    inv = x_inv[:, lanes]
+
+    def store(b, _):
+        for u in range(SLICE):
             tall[0, half, tile_at(b, u), :] = (x[half, b, u].astype(F32) - mean) * inv
         return 0
 
     lax.fori_loop(0, DAP, store, 0)
-
-
-def mid_mix(half, cot, normed, weights, tall, from_gate, grads):
-    lanes = slice(half * 128, (half + 1) * 128)
 
     def step(i, carry):
         gate_grad, out_grad = carry
         xn = tall.at[0, half][pl.ds(i, C, stride=PITCH), :].astype(BF16)
-        nb = normed[i, lanes, :]
-        gate = jax.nn.sigmoid(nn(nb, weights[2]))
         projected = tn(xn, weights[3])
+        g = gate[i, lanes, :]
         up = cot[i, lanes, :].astype(F32)
-        grad_proj = (up * gate).astype(BF16)
-        grad_logit = (up * projected * gate * (1.0 - gate)).astype(BF16)
-        gate_grad = gate_grad + tn(nb, grad_logit)
-        out_grad = out_grad + nn(xn, grad_proj)
-        tall.at[1, half][pl.ds(i, C, stride=PITCH), :] = nt(weights[3], grad_proj)
-        from_gate[i, lanes, :] = nt(grad_logit, weights[2])
+        grad_logit = (up * projected * g * (1.0 - g)).astype(BF16)
+        from_gate[i, lanes, :] = nn(grad_logit, gate_t[...])
+        gate_grad = gate_grad + nn(normed_t[half, i], grad_logit)
+        out_grad = out_grad + nn(xn, grad_proj[i, lanes, :])
         return gate_grad, out_grad
 
     zero = jnp.zeros((C, C), F32)
-    gate_grad, out_grad = lax.fori_loop(0, ROWS, step, (zero, zero), unroll=2)
-    if half == 0:
-        grads[2] = gate_grad
-        grads[3] = out_grad
-    else:
-        grads[2] = grads[2] + gate_grad
-        grads[3] = grads[3] + out_grad
-
-
-def mid_back(half, tall, x_inv, dst):
-    lanes = slice(half * 128, (half + 1) * 128)
-
-    def total(b, acc):
-        first, second = acc
-        for u in range(SLICE):
-            h = tall[1, half, tile_at(b, u), :]
-            first = first + h
-            second = second + h * tall[0, half, tile_at(b, u), :]
-        return first, second
-
-    zero = jnp.zeros((ROWS, 128), F32)
-    first, second = lax.fori_loop(0, DAP, total, (zero, zero))
-    first = first * (1.0 / C)
-    second = second * (1.0 / C)
-    inv = x_inv[:, lanes]
-
-    def store(b, _):
-        for u in range(SLICE):
-            at = tile_at(b, u)
-            v = inv * (tall[1, half, at, :] - first - tall[0, half, at, :] * second)
-            dst[half, b, u] = v.astype(BF16)
-        return 0
-
-    lax.fori_loop(0, DAP, store, 0)
+    new = lax.fori_loop(0, ROWS, step, (zero, zero), unroll=4)
+    for w in range(2):
+        grads[2 + w] = new[w] if half == 0 else grads[2 + w] + new[w]
 
 
 def grad_of_left(half, grad, right, dst):
@@ -258,24 +262,17 @@
     lax.fori_loop(0, DAP, step, 0)
 
 
-def both_sides(half, i, tall):
-    return jnp.concatenate(
-        [tall.at[w, half][pl.ds(i, C, stride=PITCH), :].astype(BF16) for w in range(2)], axis=0
-    )
-
-
-def last_grads(half, tall, normed, both, grads):
+def last_grads(half, w, tall, normed, both, grads):
     lanes = slice(half * 128, (half + 1) * 128)
+    rows = slice(w * C, (w + 1) * C)
 
     def step(i, acc):
-        pair = both_sides(half, i, tall)
-        both[i] = pair
-        return acc + nn(pair, normed[i, lanes, :])
-
-    acc = lax.fori_loop(0, ROWS, step, jnp.zeros((2 * C, C), F32), unroll=4)
-    for w in range(2):
-        new = acc[w * C : (w + 1) * C].T
-        grads[w] = new if half == 0 else grads[w] + new
+        side = tall.at[w, half][pl.ds(i, C, stride=PITCH), :].astype(BF16)
+        both[i, rows, :] = side
+        return acc + nn(side, normed[i, lanes, :])
+
+    acc = lax.fori_loop(0, ROWS, step, jnp.zeros((C, C), F32), unroll=8).T
+    grads[w] = acc if half == 0 else grads[w] + acc
 
 
 def last_pair(half, both, z_hat, z_inv, from_gate, lr, out):
@@ -383,7 +380,8 @@
 def main_kernel(
     pair_in, cot_in, error_at, q_at, residue, weights, out, update, error_out,
     pair, cot, error_in, q_init,
-    grads, mask, lr_t, lr, normed, z_hat, z_inv, from_gate, x_inv, tall, both,
+    grads, mask, lr_t, lr, gate_t, normed, normed_t, gate, grad_proj, z_hat, z_inv, from_gate,
+    h_mean, x_mean, x_inv, tall, both,
     send_l, send_r, left, right, prod, x, send_g, grad, to_l, to_r, got_l, got_r,
     part16, got16, crop16, chunk, got32, mean,
     fetch, send, recv, send_c, recv_c,
@@ -402,7 +400,7 @@
         copy.start()
         fetched.append(copy)
     greet()
-    set_up(residue, weights, mask, lr_t, lr)
+    set_up(residue, weights, mask, lr_t, lr, gate_t)
     started = []
 
     def begin(k, half, src, dst):
@@ -415,7 +413,7 @@
     sides = [(send_l, left), (send_r, right)]
     for half in range(2):
         fetched[half].wait()
-        front(half, pair, lr_t, normed, z_hat, z_inv, tall)
+        front(half, pair, lr_t, normed, normed_t, z_hat, z_inv, tall)
         for w, (src, dst) in enumerate(sides):
             pack(tall, w, half, mask, src)
             if half == 0 and w == 0:
@@ -424,6 +422,8 @@
     for copy in fetched[2:]:
         copy.wait()
     for half in range(2):
+        gating(half, cot, normed, weights, gate, grad_proj, tall, h_mean)
+    for half in range(2):
         for w in range(2):
             arrive(w, half, sides[w][1])
     for half in range(2):
@@ -431,10 +431,12 @@
         begin(2, half, prod, x)
     for half in range(2):
         arrive(2, half, x)
-        mid_norm(x, half, tall, x_inv)
-        mid_mix(half, cot, normed, weights, tall, from_gate, grads)
-        mid_back(half, tall, x_inv, send_g)
+        mid_core(half, x, tall, h_mean, x_mean, x_inv, send_g)
         begin(3, half, send_g, grad)
+        mid_rest(
+            half, x, x_mean, x_inv, cot, normed_t, gate, grad_proj, weights, gate_t,
+            tall, from_gate, grads,
+        )
     for half in range(2):
         arrive(3, half, grad)
     for half in range(2):
@@ -446,7 +448,7 @@
         for w, src in enumerate([got_l, got_r]):
             arrive(4 + w, half, src)
             unpack(src, w, half, mask, tall)
-        last_grads(half, tall, normed, both, grads)
+            last_grads(half, w, tall, normed, both, grads)
         if half == 0:
             last_pair(half, both, z_hat, z_inv, from_gate, lr, out)
     compress(
@@ -484,10 +486,16 @@
             pltpu.VMEM((ROWS, N), F32),
             pltpu.VMEM((2 * C, C), BF16),
             pltpu.VMEM((C, 2 * C), BF16),
+            pltpu.VMEM((C, C), BF16),
+            half_wide,
+            pltpu.VMEM((2, ROWS, C, 128), BF16),
+            wide,
             half_wide,
             wide,
             wide,
             wide,
+            pltpu.VMEM((ROWS, N), F32),
+            pltpu.VMEM((ROWS, N), F32),
             pltpu.VMEM((ROWS, N), F32),
             pltpu.VMEM((2, 2, C * PITCH, 128), F32),
             pltpu.VMEM((ROWS, 2 * C, 128), BF16),

time: 114 us -> 107 us (0.939)
  Pallas kernels: 113 us -> 106 us
    pallas_call x1, Pallas kernels: 112 us -> 105 us  [main_call(): pl.pallas_call(main_kernel, name='triangle', out_shape=(pltpu.VMEM((ROWS,...]
where the time goes in v3:
time: 107 us
  Pallas kernels  106 us (99%)
    pallas_call x1, Pallas kernels, main_call(): pl.pallas_call(main_kernel, name='triangle', out_shape=(pltpu.VMEM((ROWS,...  105 us

profile of v3, /device:TPU:1, one launch (start us, length us, event | category | flops | bytes accessed | tf_op | source)
XLA Modules:
  0.0 106.7 jit_solution(12619949835118088278)
XLA Ops:
  0.6 104.9 %triangle.1 = (bf16[16,256,128]{2,1,0:T(8,128)(2,1)S(1)}, f32[4,128,128]{2,1,0:T(8,128)S(1)}, f32[4,128,128]{2,1,0:T(8,128)S(1)}) custom-call(bf16[16,256,128]{2,1,0:T(8,128)(2,1)} %bitcast.6, bf16[16,256,128]{2,1,0:T(8,128)(2,1)} %bitcast.7, f32[4,128,128]{2,1,0:T(8,128)} %bitcast.8, f32[4,32,128]{2,1,0:T(8,128)} %bitcast.9, s32[1,256]{1,0:T(1,128)} %residue.1, ...), custom_call_target="tpu_custom_call" | custom-call | tf_op jit(solution)/shard_map/triangle/pallas_call | solution.py:470
  105.6 1.2 %store.1 = (bf16[16,256,128]{2,1,0:T(8,128)(2,1)}, f32[4,128,128]{2,1,0:T(8,128)}, f32[4,128,128]{2,1,0:T(8,128)}) custom-call(bf16[16,256,128]{2,1,0:T(8,128)(2,1)S(1)} %get-tuple-element.9.refs_0_, f32[4,128,128]{2,1,0:T(8,128)S(1)} %get-tuple-element.10.refs_1_, f32[4,128,128]{2,1,0:T(8,128)S(1)} %get-tuple-element.11.refs_2_), custom_call_target="tpu_custom_call" | custom-call | tf_op jit(solution)/shard_map/store/pallas_call | solution.py:538

commit v4 on v3

--- a/solution.py
+++ b/solution.py
@@ -16,10 +16,12 @@
 N = 256
 ROWS = 16
 SLICE = 8
+GROUP = 4
 PITCH = 17
 RANK = 32
 DAP = 16
 DP = 8
+PART = 2 * C // DAP
 OFFSETS = [(2,2),(1,2),(3,2),(2,1),(2,3),(1,1),(3,3),(1,3),(3,1),(2,0),(0,2),(1,0),(3,0),(0,1),(0,3)]
 
 
@@ -29,6 +31,11 @@
 
 def nt(a, b):
     return lax.dot_general(a, b, (((1,), (1,)), ((), ())), preferred_element_type=F32)
+
+
+def exact(a, b, a_dim, b_dim):
+    dims = (((a_dim,), (b_dim,)), ((), ()))
+    return lax.dot_general(a, b, dims, preferred_element_type=F32, precision=HIGH)
 
 
 def tn(a, b):
@@ -68,11 +75,15 @@
     return copy
 
 
-def exchange(src, dst, half, send, recv):
+def exchange(src, dst, half, group, send, recv):
     me = lax.axis_index("dap")
+    these = pl.ds(group * GROUP, GROUP)
     for peer in peers():
-        remote(src.at[half, peer], dst.at[half, me], send.at[half], recv.at[half], "dap", peer)
-    pltpu.make_async_copy(src.at[half, me], dst.at[half, me], recv.at[half]).start()
+        remote(
+            src.at[half, peer, these], dst.at[half, me, these],
+            send.at[half], recv.at[half, group], "dap", peer,
+        )
+    pltpu.make_async_copy(src.at[half, me, these], dst.at[half, me, these], recv.at[half, group]).start()
 
 
 def await_bytes(ref, sem):
@@ -159,14 +170,14 @@
     return jnp.concatenate([plane(ref, 0, c), plane(ref, 1, c)], axis=1)
 
 
-def first_triangle(half, left, right, prod):
+def first_triangle(half, group, left, right, prod):
     def step(c, _):
         cols = right[:, half * DAP // 2 : (half + 1) * DAP // 2, c]
         cols = jnp.concatenate([cols[0].reshape(128, 128), cols[1].reshape(128, 128)], axis=1)
         prod[half, :, c] = nt(whole(left, c), cols).astype(BF16).reshape(DAP, ROWS, 128)
         return 0
 
-    lax.fori_loop(0, SLICE, step, 0, unroll=4)
+    lax.fori_loop(group * GROUP, (group + 1) * GROUP, step, 0, unroll=4)
 
 
 def mid_core(half, x, tall, h_mean, x_mean, x_inv, dst):
@@ -235,20 +246,20 @@
         grads[2 + w] = new[w] if half == 0 else grads[2 + w] + new[w]
 
 
-def grad_of_left(half, grad, right, dst):
+def grad_of_left(half, group, grad, right, dst):
     def step(c, _):
         dst[half, :, c] = nn(whole(grad, c), plane(right, half, c)).astype(BF16).reshape(DAP, ROWS, 128)
         return 0
 
-    lax.fori_loop(0, SLICE, step, 0, unroll=4)
-
-
-def grad_of_right(half, grad, left, dst):
+    lax.fori_loop(group * GROUP, (group + 1) * GROUP, step, 0, unroll=4)
+
+
+def grad_of_right(half, group, grad, left, dst):
     def step(c, _):
         dst[half, :, c] = tn(whole(grad, c), plane(left, half, c)).astype(BF16).reshape(DAP, ROWS, 128)
         return 0
 
-    lax.fori_loop(0, SLICE, step, 0, unroll=4)
+    lax.fori_loop(group * GROUP, (group + 1) * GROUP, step, 0, unroll=4)
 
 
 def unpack(src, w, half, mask, tall):
@@ -313,68 +324,74 @@
     ]
 
 
-def compress(grads, error_in, q_init, update, error_out, bufs, sems, meanwhile):
-    part16, got16, crop16, chunk, got32, mean = bufs
-    send, recv = sems
-    me, dp = lax.axis_index("dap"), lax.axis_index("dp")
-    rows = 4 * C // DAP
-    mine = pl.ds(pl.multiple_of(me * rows, rows), rows)
-    others = peers()
-
-    for w in range(4):
-        part16[w * C : (w + 1) * C, :] = grads[w].astype(BF16)
-    for t, peer in enumerate(others):
-        block = part16.at[pl.ds(pl.multiple_of(peer * rows, rows), rows)]
-        remote(block, got16.at[t], send.at[0], recv.at[0], "dap", peer)
-    meanwhile()
-    await_bytes(got16, recv.at[0])
-    total = part16[mine, :].astype(F32)
-    for t in range(DAP - 1):
-        total = total + got16[t].astype(F32)
-    crop16[mine, :] = (total * (1.0 / N)).astype(BF16)
-
-    matrix, first = me // 4, pl.multiple_of(lax.rem(me, 4) * rows, rows)
-    chunk[...] = crop16[mine, :].astype(F32) + error_in[matrix, pl.ds(first, rows), :]
-    got32[dp] = chunk[...]
-    for s in range(1, DP):
-        remote(chunk, got32.at[dp], send.at[1], recv.at[1], "dp", lax.rem(dp + s, DP))
-    for peer in others:
-        remote(crop16.at[mine], crop16.at[mine], send.at[2], recv.at[2], "dap", peer)
-    await_bytes(got32.at[pl.ds(0, DP - 1)], recv.at[1])
-    total = got32[0]
-    for r in range(1, DP):
-        total = total + got32[r]
-    mean[mine, :] = total * (1.0 / DP)
-    for peer in others:
-        remote(mean.at[mine], mean.at[mine], send.at[3], recv.at[3], "dap", peer)
-    gathered = pl.ds(0, 4 * C - rows)
-    await_bytes(mean.at[gathered], recv.at[3])
-
-    panel = []
-    for w in range(4):
-        rows_of = lax.dot_general(
-            q_init[w], mean[w * C : (w + 1) * C, :], (((1,), (1,)), ((), ())),
-            preferred_element_type=F32, precision=HIGH,
-        )
-        panel.append([rows_of[t * 8 : (t + 1) * 8, :] for t in range(RANK // 8)])
-    basis = gram_schmidt(panel)
-    await_bytes(crop16.at[gathered], recv.at[2])
-    for w in range(4):
-        here = slice(w * C, (w + 1) * C)
-        coeffs = lax.dot_general(
-            basis[w], mean[here, :], (((1,), (0,)), ((), ())),
-            preferred_element_type=F32, precision=HIGH,
-        )
-        new = lax.dot_general(
-            basis[w], coeffs, (((0,), (0,)), ((), ())),
-            preferred_element_type=F32, precision=HIGH,
-        )
-        update[w] = new
-        error_out[w] = crop16[here, :].astype(F32) + error_in[w] - new
-    await_bytes(part16.at[gathered], send.at[0])
-    await_bytes(got32.at[pl.ds(0, DP - 1)], send.at[1])
-    await_bytes(crop16.at[gathered], send.at[2])
-    await_bytes(mean.at[gathered], send.at[3])
+class Compression:
+    def __init__(self, first, refs, grads, error_in, q_init, update, error_out):
+        self.first = first
+        self.part16, self.got16, self.crop16, self.chunk, self.got32, self.mean, self.send, self.recv = refs
+        self.grads, self.error_in, self.q_init = grads, error_in, q_init
+        self.update, self.error_out = update, error_out
+        self.me, self.dp = lax.axis_index("dap"), lax.axis_index("dp")
+        self.mine = pl.ds(pl.multiple_of(self.me * PART, PART), PART)
+        self.others = pl.ds(0, 2 * C - PART)
+        self.replicas = pl.ds(0, DP - 1)
+
+    def scatter(self):
+        for w in range(2):
+            self.part16[w * C : (w + 1) * C, :] = self.grads[self.first + w].astype(BF16)
+        for t, peer in enumerate(peers()):
+            block = self.part16.at[pl.ds(pl.multiple_of(peer * PART, PART), PART)]
+            remote(block, self.got16.at[t], self.send.at[0], self.recv.at[0], "dap", peer)
+
+    def across(self):
+        await_bytes(self.got16, self.recv.at[0])
+        total = self.part16[self.mine, :].astype(F32)
+        for t in range(DAP - 1):
+            total = total + self.got16[t].astype(F32)
+        self.crop16[self.mine, :] = (total * (1.0 / N)).astype(BF16)
+        matrix = self.first + self.me // 8
+        row = pl.multiple_of(lax.rem(self.me, 8) * PART, PART)
+        self.chunk[...] = self.crop16[self.mine, :].astype(F32) + self.error_in[matrix, pl.ds(row, PART), :]
+        self.got32[self.dp] = self.chunk[...]
+        for s in range(1, DP):
+            peer = lax.rem(self.dp + s, DP)
+            remote(self.chunk, self.got32.at[self.dp], self.send.at[1], self.recv.at[1], "dp", peer)
+
+    def share(self):
+        for peer in peers():
+            block = self.crop16.at[self.mine]
+            remote(block, block, self.send.at[2], self.recv.at[2], "dap", peer)
+
+    def gather(self):
+        await_bytes(self.got32.at[self.replicas], self.recv.at[1])
+        total = self.got32[0]
+        for r in range(1, DP):
+            total = total + self.got32[r]
+        self.mean[self.mine, :] = total * (1.0 / DP)
+        for peer in peers():
+            block = self.mean.at[self.mine]
+            remote(block, block, self.send.at[3], self.recv.at[3], "dap", peer)
+
+    def finish(self):
+        await_bytes(self.mean.at[self.others], self.recv.at[3])
+        panel = []
+        for w in range(2):
+            rows = exact(self.q_init[self.first + w], self.mean[w * C : (w + 1) * C, :], 1, 1)
+            panel.append([rows[t * 8 : (t + 1) * 8, :] for t in range(RANK // 8)])
+        basis = gram_schmidt(panel)
+        await_bytes(self.crop16.at[self.others], self.recv.at[2])
+        for w in range(2):
+            here = slice(w * C, (w + 1) * C)
+            coeffs = exact(basis[w], self.mean[here, :], 1, 0)
+            new = exact(basis[w], coeffs, 0, 0)
+            self.update[self.first + w] = new
+            memory = self.crop16[here, :].astype(F32) + self.error_in[self.first + w]
+            self.error_out[self.first + w] = memory - new
+
+    def sent(self):
+        await_bytes(self.part16.at[self.others], self.send.at[0])
+        await_bytes(self.got32.at[self.replicas], self.send.at[1])
+        await_bytes(self.crop16.at[self.others], self.send.at[2])
+        await_bytes(self.mean.at[self.others], self.send.at[3])
 
 
 def main_kernel(
@@ -383,9 +400,11 @@
     grads, mask, lr_t, lr, gate_t, normed, normed_t, gate, grad_proj, z_hat, z_inv, from_gate,
     h_mean, x_mean, x_inv, tall, both,
     send_l, send_r, left, right, prod, x, send_g, grad, to_l, to_r, got_l, got_r,
-    part16, got16, crop16, chunk, got32, mean,
-    fetch, send, recv, send_c, recv_c,
+    fetch, send, recv, *shared,
 ):
+    size = len(shared) // 2
+    late = Compression(0, shared[:size], grads, error_in, q_init, update, error_out)
+    early = Compression(2, shared[size:], grads, error_in, q_init, update, error_out)
     fetched = []
     for k, (src, dst) in enumerate(
         [
@@ -403,12 +422,13 @@
     set_up(residue, weights, mask, lr_t, lr, gate_t)
     started = []
 
-    def begin(k, half, src, dst):
-        exchange(src, dst, half, send.at[k], recv.at[k])
-        started.append((src, half, k))
-
-    def arrive(k, half, dst):
-        await_bytes(dst.at[half], recv.at[k, half])
+    def begin(k, half, group, src, dst):
+        exchange(src, dst, half, group, send.at[k], recv.at[k])
+        if group == 0:
+            started.append((src, half, k))
+
+    def arrive(k, half, group, dst):
+        await_bytes(dst.at[half, :, pl.ds(group * GROUP, GROUP)], recv.at[k, half, group])
 
     sides = [(send_l, left), (send_r, right)]
     for half in range(2):
@@ -418,44 +438,69 @@
             pack(tall, w, half, mask, src)
             if half == 0 and w == 0:
                 greeted()
-            begin(w, half, src, dst)
+            begin(w, half, 0, src, dst)
+    for half in range(2):
+        for w, (src, dst) in enumerate(sides):
+            begin(w, half, 1, src, dst)
     for copy in fetched[2:]:
         copy.wait()
     for half in range(2):
         gating(half, cot, normed, weights, gate, grad_proj, tall, h_mean)
+    for group in range(2):
+        for half in range(2):
+            for w in range(2):
+                arrive(w, half, group, sides[w][1])
+        first_triangle(0, group, left, right, prod)
+        begin(2, 0, group, prod, x)
+    for group in range(2):
+        first_triangle(1, group, left, right, prod)
+        begin(2, 1, group, prod, x)
     for half in range(2):
-        for w in range(2):
-            arrive(w, half, sides[w][1])
-    for half in range(2):
-        first_triangle(half, left, right, prod)
-        begin(2, half, prod, x)
-    for half in range(2):
-        arrive(2, half, x)
+        for group in range(2):
+            arrive(2, half, group, x)
         mid_core(half, x, tall, h_mean, x_mean, x_inv, send_g)
-        begin(3, half, send_g, grad)
+        for group in range(2):
+            begin(3, half, group, send_g, grad)
         mid_rest(
             half, x, x_mean, x_inv, cot, normed_t, gate, grad_proj, weights, gate_t,
             tall, from_gate, grads,
         )
-    for half in range(2):
-        arrive(3, half, grad)
-    for half in range(2):
-        grad_of_left(half, grad, right, to_l)
-        begin(4, half, to_l, got_l)
-        grad_of_right(half, grad, left, to_r)
-        begin(5, half, to_r, got_r)
+    early.scatter()
+    for group in range(2):
+        for half in range(2):
+            arrive(3, half, group, grad)
+        grad_of_left(0, group, grad, right, to_l)
+        begin(4, 0, group, to_l, got_l)
+        grad_of_right(0, group, grad, left, to_r)
+        begin(5, 0, group, to_r, got_r)
+    for k in range(2):
+        for group in range(2):
+            if k == 0:
+                grad_of_left(1, group, grad, right, to_l)
+                begin(4, 1, group, to_l, got_l)
+            else:
+                grad_of_right(1, group, grad, left, to_r)
+                begin(5, 1, group, to_r, got_r)
+    early.across()
     for half in range(2):
         for w, src in enumerate([got_l, got_r]):
-            arrive(4 + w, half, src)
+            for group in range(2):
+                arrive(4 + w, half, group, src)
             unpack(src, w, half, mask, tall)
             last_grads(half, w, tall, normed, both, grads)
         if half == 0:
             last_pair(half, both, z_hat, z_inv, from_gate, lr, out)
-    compress(
-        grads, error_in, q_init, update, error_out,
-        (part16, got16, crop16, chunk, got32, mean), (send_c, recv_c),
-        lambda: last_pair(1, both, z_hat, z_inv, from_gate, lr, out),
-    )
+    late.scatter()
+    early.gather()
+    early.share()
+    last_pair(1, both, z_hat, z_inv, from_gate, lr, out)
+    late.across()
+    late.gather()
+    late.share()
+    early.finish()
+    late.finish()
+    late.sent()
+    early.sent()
     for src, half, k in started:
         await_bytes(src.at[half, pl.ds(0, DAP - 1)], send.at[k, half])
 
@@ -466,7 +511,6 @@
     blocks = pltpu.VMEM((2, DAP, SLICE, ROWS, 128), BF16)
     wide = pltpu.VMEM((ROWS, N, C), F32)
     half_wide = pltpu.VMEM((ROWS, N, C), BF16)
-    part = 4 * C // DAP
     return pl.pallas_call(
         main_kernel,
         name="triangle",
@@ -502,18 +546,21 @@
         ]
         + [blocks] * 12
         + [
-            pltpu.VMEM((4 * C, C), BF16),
-            pltpu.VMEM((DAP - 1, part, C), BF16),
-            pltpu.VMEM((4 * C, C), BF16),
-            pltpu.VMEM((part, C), F32),
-            pltpu.VMEM((DP, part, C), F32),
-            pltpu.VMEM((4 * C, C), F32),
             pltpu.SemaphoreType.DMA((5,)),
             pltpu.SemaphoreType.DMA((6, 2)),
-            pltpu.SemaphoreType.DMA((6, 2)),
+            pltpu.SemaphoreType.DMA((6, 2, 2)),
+        ]
+        + [
+            pltpu.VMEM((2 * C, C), BF16),
+            pltpu.VMEM((DAP - 1, PART, C), BF16),
+            pltpu.VMEM((2 * C, C), BF16),
+            pltpu.VMEM((PART, C), F32),
+            pltpu.VMEM((DP, PART, C), F32),
+            pltpu.VMEM((2 * C, C), F32),
             pltpu.SemaphoreType.DMA((4,)),
             pltpu.SemaphoreType.DMA((4,)),
-        ],
+        ]
+        * 2,
         compiler_params=pltpu.CompilerParams(
             collective_id=0, has_side_effects=True, vmem_limit_bytes=56 << 20
         ),

time: 107 us -> 101 us (0.944)
  Pallas kernels: 106 us -> 100 us
    pallas_call x1, Pallas kernels: 105 us -> 99 us  [main_call(): pl.pallas_call(main_kernel, name='triangle', out_shape=(pltpu.VMEM((ROWS,...]
where the time goes in v4:
time: 101 us
  Pallas kernels  100 us (99%)
    pallas_call x1, Pallas kernels, main_call(): pl.pallas_call(main_kernel, name='triangle', out_shape=(pltpu.VMEM((ROWS,...  99 us

profile of v4, /device:TPU:1, one launch (start us, length us, event | category | flops | bytes accessed | tf_op | source)
XLA Modules:
  0.0 100.8 jit_solution(15599900084848572699)
XLA Ops:
  0.6 99.0 %triangle.1 = (bf16[16,256,128]{2,1,0:T(8,128)(2,1)S(1)}, f32[4,128,128]{2,1,0:T(8,128)S(1)}, f32[4,128,128]{2,1,0:T(8,128)S(1)}) custom-call(bf16[16,256,128]{2,1,0:T(8,128)(2,1)} %bitcast.6, bf16[16,256,128]{2,1,0:T(8,128)(2,1)} %bitcast.7, f32[4,128,128]{2,1,0:T(8,128)} %bitcast.8, f32[4,32,128]{2,1,0:T(8,128)} %bitcast.9, s32[1,256]{1,0:T(1,128)} %residue.1, ...), custom_call_target="tpu_custom_call" | custom-call | tf_op jit(solution)/shard_map/triangle/pallas_call | solution.py:514
  99.7 1.2 %store.1 = (bf16[16,256,128]{2,1,0:T(8,128)(2,1)}, f32[4,128,128]{2,1,0:T(8,128)}, f32[4,128,128]{2,1,0:T(8,128)}) custom-call(bf16[16,256,128]{2,1,0:T(8,128)(2,1)S(1)} %get-tuple-element.9.refs_0_, f32[4,128,128]{2,1,0:T(8,128)S(1)} %get-tuple-element.10.refs_1_, f32[4,128,128]{2,1,0:T(8,128)S(1)} %get-tuple-element.11.refs_2_), custom_call_target="tpu_custom_call" | custom-call | tf_op jit(solution)/shard_map/store/pallas_call | solution.py:585

commit v5 on v4

--- a/solution.py
+++ b/solution.py
@@ -17,6 +17,7 @@
 ROWS = 16
 SLICE = 8
 GROUP = 4
+AHEAD = 3
 PITCH = 17
 RANK = 32
 DAP = 16
@@ -77,13 +78,13 @@
 
 def exchange(src, dst, half, group, send, recv):
     me = lax.axis_index("dap")
-    these = pl.ds(group * GROUP, GROUP)
+    these = pl.ds(0, SLICE) if group is None else pl.ds(group * GROUP, GROUP)
+    arrived = recv.at[half, group or 0]
     for peer in peers():
         remote(
-            src.at[half, peer, these], dst.at[half, me, these],
-            send.at[half], recv.at[half, group], "dap", peer,
+            src.at[half, peer, these], dst.at[half, me, these], send.at[half], arrived, "dap", peer
         )
-    pltpu.make_async_copy(src.at[half, me, these], dst.at[half, me, these], recv.at[half, group]).start()
+    pltpu.make_async_copy(src.at[half, me, these], dst.at[half, me, these], arrived).start()
 
 
 def await_bytes(ref, sem):
@@ -106,23 +107,28 @@
 def front(half, pair, lr_t, normed, normed_t, z_hat, z_inv, tall):
     lanes = slice(half * 128, (half + 1) * 128)
 
-    def step(i, _):
-        x = pair[i, lanes, :].astype(F32)
-        centre = x - jnp.sum(x, axis=-1, keepdims=True) * (1.0 / C)
-        inv = lax.rsqrt(jnp.sum(centre * centre, axis=-1, keepdims=True) * (1.0 / C) + EPS)
-        z = centre * inv
-        nb = z.astype(BF16)
-        nb_t = nb.T
-        normed[i, lanes, :] = nb
-        normed_t[half, i] = nb_t
-        z_hat[i, lanes, :] = z
-        z_inv[i, lanes, :] = jnp.broadcast_to(inv, (128, C))
-        both = nn(lr_t[...], nb_t)
-        for w in range(2):
-            tall.at[w, half][pl.ds(i, C, stride=PITCH), :] = both[w * C : (w + 1) * C]
-        return 0
-
-    lax.fori_loop(0, ROWS, step, 0, unroll=4)
+    def step(p, _):
+        turned = []
+        for i in (2 * p, 2 * p + 1):
+            x = pair[i, lanes, :].astype(F32)
+            centre = x - jnp.sum(x, axis=-1, keepdims=True) * (1.0 / C)
+            inv = lax.rsqrt(jnp.sum(centre * centre, axis=-1, keepdims=True) * (1.0 / C) + EPS)
+            z = centre * inv
+            nb = z.astype(BF16)
+            turned.append(nb.T)
+            normed[i, lanes, :] = nb
+            normed_t[half, i] = turned[-1]
+            z_hat[i, lanes, :] = z
+            z_inv[i, lanes, :] = jnp.broadcast_to(inv, (128, C))
+        both = nn(lr_t[...], jnp.concatenate(turned, axis=1))
+        for u in range(2):
+            for w in range(2):
+                tall.at[w, half][pl.ds(2 * p + u, C, stride=PITCH), :] = both[
+                    w * C : (w + 1) * C, u * 128 : (u + 1) * 128
+                ]
+        return 0
+
+    lax.fori_loop(0, ROWS // 2, step, 0, unroll=4)
 
 
 def gating(half, cot, normed, weights, gate, grad_proj, tall, h_mean):
@@ -277,12 +283,15 @@
     lanes = slice(half * 128, (half + 1) * 128)
     rows = slice(w * C, (w + 1) * C)
 
-    def step(i, acc):
-        side = tall.at[w, half][pl.ds(i, C, stride=PITCH), :].astype(BF16)
-        both[i, rows, :] = side
-        return acc + nn(side, normed[i, lanes, :])
-
-    acc = lax.fori_loop(0, ROWS, step, jnp.zeros((C, C), F32), unroll=8).T
+    def step(p, acc):
+        sides = []
+        for i in (2 * p, 2 * p + 1):
+            sides.append(tall.at[w, half][pl.ds(i, C, stride=PITCH), :].astype(BF16))
+            both[i, rows, :] = sides[-1]
+        cells = jnp.concatenate([normed[2 * p, lanes, :], normed[2 * p + 1, lanes, :]], axis=0)
+        return acc + nn(jnp.concatenate(sides, axis=1), cells)
+
+    acc = lax.fori_loop(0, ROWS // 2, step, jnp.zeros((C, C), F32), unroll=4).T
     grads[w] = acc if half == 0 else grads[w] + acc
 
 
@@ -301,27 +310,29 @@
 
 
 def gram_schmidt(panel):
-    row = lax.broadcasted_iota(jnp.int32, (8, 1), 0)
+    lane = lax.broadcasted_iota(jnp.int32, (1, C), 1)
+    within = lax.rem(lane, RANK)
+
+    def spread(j):
+        return jnp.where(
+            lane < RANK,
+            jnp.broadcast_to(panel[:, j : j + 1], (C, C)),
+            jnp.broadcast_to(panel[:, RANK + j : RANK + j + 1], (C, C)),
+        )
+
+    coming = {j: spread(j) for j in range(AHEAD + 1)}
     for j in range(RANK):
-        at, sub = j // 8, j % 8
-        for tiles in panel:
-            v = jnp.broadcast_to(tiles[at][sub : sub + 1, :], (8, C))
-            dots = [
-                jnp.sum(tiles[t] * v, axis=1, keepdims=True) if t >= at else None
-                for t in range(RANK // 8)
-            ]
-            scale = 1.0 / jnp.broadcast_to(dots[at][sub : sub + 1, :], (8, 1))
-            for t in range(at, RANK // 8):
-                coef = dots[t] * scale
-                if t == at:
-                    coef = jnp.where(row > sub, coef, 0.0)
-                tiles[t] = tiles[t] - coef * v
-    return [
-        jnp.concatenate(
-            [t * lax.rsqrt(jnp.sum(t * t, axis=1, keepdims=True)) for t in tiles], axis=0
-        )
-        for tiles in panel
-    ]
+        v = coming.pop(j)
+        per = 1.0 / jnp.sum(v * v, axis=0, keepdims=True)
+        for k in list(coming):
+            alpha = jnp.sum(coming[k] * v, axis=0, keepdims=True) * per
+            coming[k] = coming[k] - alpha * v
+        on_v = jnp.sum(panel * v, axis=0, keepdims=True) * per
+        panel = panel - jnp.where(within > j, on_v, 0.0) * v
+        if j + AHEAD + 1 < RANK:
+            coming[j + AHEAD + 1] = spread(j + AHEAD + 1)
+    unit = panel * lax.rsqrt(jnp.sum(panel * panel, axis=0, keepdims=True))
+    return jnp.where(lane < 2 * RANK, unit, 0.0)
 
 
 class Compression:
@@ -373,16 +384,17 @@
 
     def finish(self):
         await_bytes(self.mean.at[self.others], self.recv.at[3])
-        panel = []
-        for w in range(2):
-            rows = exact(self.q_init[self.first + w], self.mean[w * C : (w + 1) * C, :], 1, 1)
-            panel.append([rows[t * 8 : (t + 1) * 8, :] for t in range(RANK // 8)])
+        panel = sum(
+            exact(self.mean[w * C : (w + 1) * C, :], self.q_init[self.first + w], 1, 0) for w in range(2)
+        )
         basis = gram_schmidt(panel)
+        rows = basis.T
+        lane = lax.broadcasted_iota(jnp.int32, (1, C), 1)
         await_bytes(self.crop16.at[self.others], self.recv.at[2])
         for w in range(2):
             here = slice(w * C, (w + 1) * C)
-            coeffs = exact(basis[w], self.mean[here, :], 1, 0)
-            new = exact(basis[w], coeffs, 0, 0)
+            coeffs = exact(rows, self.mean[here, :], 1, 0)
+            new = exact(jnp.where(lane // RANK == w, basis, 0.0), coeffs, 1, 0)
             self.update[self.first + w] = new
             memory = self.crop16[here, :].astype(F32) + self.error_in[self.first + w]
             self.error_out[self.first + w] = memory - new
@@ -396,15 +408,15 @@
 
 def main_kernel(
     pair_in, cot_in, error_at, q_at, residue, weights, out, update, error_out,
-    pair, cot, error_in, q_init,
+    pair, cot, error_in, q_init, q_wide,
     grads, mask, lr_t, lr, gate_t, normed, normed_t, gate, grad_proj, z_hat, z_inv, from_gate,
     h_mean, x_mean, x_inv, tall, both,
     send_l, send_r, left, right, prod, x, send_g, grad, to_l, to_r, got_l, got_r,
     fetch, send, recv, *shared,
 ):
     size = len(shared) // 2
-    late = Compression(0, shared[:size], grads, error_in, q_init, update, error_out)
-    early = Compression(2, shared[size:], grads, error_in, q_init, update, error_out)
+    late = Compression(0, shared[:size], grads, error_in, q_wide, update, error_out)
+    early = Compression(2, shared[size:], grads, error_in, q_wide, update, error_out)
     fetched = []
     for k, (src, dst) in enumerate(
         [
@@ -424,11 +436,12 @@
 
     def begin(k, half, group, src, dst):
         exchange(src, dst, half, group, send.at[k], recv.at[k])
-        if group == 0:
+        if not group:
             started.append((src, half, k))
 
     def arrive(k, half, group, dst):
-        await_bytes(dst.at[half, :, pl.ds(group * GROUP, GROUP)], recv.at[k, half, group])
+        these = pl.ds(0, SLICE) if group is None else pl.ds(group * GROUP, GROUP)
+        await_bytes(dst.at[half, :, these], recv.at[k, half, group or 0])
 
     sides = [(send_l, left), (send_r, right)]
     for half in range(2):
@@ -444,6 +457,11 @@
             begin(w, half, 1, src, dst)
     for copy in fetched[2:]:
         copy.wait()
+    for w in range(4):
+        parts = [q_init[w], jnp.zeros((C - RANK, C), F32)]
+        if w % 2:
+            parts = [jnp.zeros((RANK, C), F32), q_init[w], jnp.zeros((C - 2 * RANK, C), F32)]
+        q_wide[w] = jnp.concatenate(parts, axis=0).T
     for half in range(2):
         gating(half, cot, normed, weights, gate, grad_proj, tall, h_mean)
     for group in range(2):
@@ -454,12 +472,12 @@
         begin(2, 0, group, prod, x)
     for group in range(2):
         first_triangle(1, group, left, right, prod)
-        begin(2, 1, group, prod, x)
+    begin(2, 1, None, prod, x)
     for half in range(2):
-        for group in range(2):
+        for group in range(2) if half == 0 else [None]:
             arrive(2, half, group, x)
         mid_core(half, x, tall, h_mean, x_mean, x_inv, send_g)
-        for group in range(2):
+        for group in [None] if half == 0 else range(2):
             begin(3, half, group, send_g, grad)
         mid_rest(
             half, x, x_mean, x_inv, cot, normed_t, gate, grad_proj, weights, gate_t,
@@ -467,24 +485,23 @@
         )
     early.scatter()
     for group in range(2):
-        for half in range(2):
-            arrive(3, half, group, grad)
+        if group == 0:
+            arrive(3, 0, None, grad)
+        arrive(3, 1, group, grad)
         grad_of_left(0, group, grad, right, to_l)
         begin(4, 0, group, to_l, got_l)
         grad_of_right(0, group, grad, left, to_r)
         begin(5, 0, group, to_r, got_r)
-    for k in range(2):
-        for group in range(2):
-            if k == 0:
-                grad_of_left(1, group, grad, right, to_l)
-                begin(4, 1, group, to_l, got_l)
-            else:
-                grad_of_right(1, group, grad, left, to_r)
-                begin(5, 1, group, to_r, got_r)
+    for group in range(2):
+        grad_of_left(1, group, grad, right, to_l)
+    begin(4, 1, None, to_l, got_l)
+    for group in range(2):
+        grad_of_right(1, group, grad, left, to_r)
+    begin(5, 1, None, to_r, got_r)
     early.across()
     for half in range(2):
         for w, src in enumerate([got_l, got_r]):
-            for group in range(2):
+            for group in range(2) if half == 0 else [None]:
                 arrive(4 + w, half, group, src)
             unpack(src, w, half, mask, tall)
             last_grads(half, w, tall, normed, both, grads)
@@ -526,6 +543,7 @@
             half_wide,
             pltpu.VMEM((4, C, C), F32),
             pltpu.VMEM((4, RANK, C), F32),
+            pltpu.VMEM((4, C, C), F32),
             pltpu.VMEM((4, C, C), F32),
             pltpu.VMEM((ROWS, N), F32),
             pltpu.VMEM((2 * C, C), BF16),

time: 101 us -> 99.6 us (0.986)
  Pallas kernels: 100 us -> 98.7 us
    pallas_call x1, Pallas kernels: 99 us -> 97.5 us  [main_call(): pl.pallas_call(main_kernel, name='triangle', out_shape=(pltpu.VMEM((ROWS,...]
where the time goes in v5:
time: 99.6 us; the launch traced here: 99.5 us
  Pallas kernels  98.7 us (99%)
    pallas_call x1, Pallas kernels, main_call(): pl.pallas_call(main_kernel, name='triangle', out_shape=(pltpu.VMEM((ROWS,...  97.5 us

profile of v5, /device:TPU:1, one launch (start us, length us, event | category | flops | bytes accessed | tf_op | source)
XLA Modules:
  0.0 99.5 jit_solution(15779324993976743380)
XLA Ops:
  0.6 97.5 %triangle.1 = (bf16[16,256,128]{2,1,0:T(8,128)(2,1)S(1)}, f32[4,128,128]{2,1,0:T(8,128)S(1)}, f32[4,128,128]{2,1,0:T(8,128)S(1)}) custom-call(bf16[16,256,128]{2,1,0:T(8,128)(2,1)} %bitcast.6, bf16[16,256,128]{2,1,0:T(8,128)(2,1)} %bitcast.7, f32[4,128,128]{2,1,0:T(8,128)} %bitcast.8, f32[4,32,128]{2,1,0:T(8,128)} %bitcast.9, s32[1,256]{1,0:T(1,128)} %residue.1, ...), custom_call_target="tpu_custom_call" | custom-call | tf_op jit(solution)/shard_map/triangle/pallas_call | solution.py:531
  98.2 1.2 %store.1 = (bf16[16,256,128]{2,1,0:T(8,128)(2,1)}, f32[4,128,128]{2,1,0:T(8,128)}, f32[4,128,128]{2,1,0:T(8,128)}) custom-call(bf16[16,256,128]{2,1,0:T(8,128)(2,1)S(1)} %get-tuple-element.9.refs_0_, f32[4,128,128]{2,1,0:T(8,128)S(1)} %get-tuple-element.10.refs_1_, f32[4,128,128]{2,1,0:T(8,128)S(1)} %get-tuple-element.11.refs_2_), custom_call_target="tpu_custom_call" | custom-call | tf_op jit(solution)/shard_map/store/pallas_call | solution.py:603

commit v6 on v5

--- a/solution.py
+++ b/solution.py
@@ -363,7 +363,7 @@
         row = pl.multiple_of(lax.rem(self.me, 8) * PART, PART)
         self.chunk[...] = self.crop16[self.mine, :].astype(F32) + self.error_in[matrix, pl.ds(row, PART), :]
         self.got32[self.dp] = self.chunk[...]
-        for s in range(1, DP):
+        for s in (4, 5, 3, 6, 2, 7, 1):
             peer = lax.rem(self.dp + s, DP)
             remote(self.chunk, self.got32.at[self.dp], self.send.at[1], self.recv.at[1], "dp", peer)
 

time: 99.6 us -> 99.4 us (level)
  no operation moved by 1% of the time
where the time goes in v6:
time: 99.4 us; the launch traced here: 99.3 us
  Pallas kernels  98.5 us (99%)
    pallas_call x1, Pallas kernels, main_call(): pl.pallas_call(main_kernel, name='triangle', out_shape=(pltpu.VMEM((ROWS,...  97.3 us

profile of v6, /device:TPU:1, one launch (start us, length us, event | category | flops | bytes accessed | tf_op | source)
XLA Modules:
  0.0 99.3 jit_solution(1241471750324355753)
XLA Ops:
  0.6 97.3 %triangle.1 = (bf16[16,256,128]{2,1,0:T(8,128)(2,1)S(1)}, f32[4,128,128]{2,1,0:T(8,128)S(1)}, f32[4,128,128]{2,1,0:T(8,128)S(1)}) custom-call(bf16[16,256,128]{2,1,0:T(8,128)(2,1)} %bitcast.6, bf16[16,256,128]{2,1,0:T(8,128)(2,1)} %bitcast.7, f32[4,128,128]{2,1,0:T(8,128)} %bitcast.8, f32[4,32,128]{2,1,0:T(8,128)} %bitcast.9, s32[1,256]{1,0:T(1,128)} %residue.1, ...), custom_call_target="tpu_custom_call" | custom-call | tf_op jit(solution)/shard_map/triangle/pallas_call | solution.py:531
  98.0 1.2 %store.1 = (bf16[16,256,128]{2,1,0:T(8,128)(2,1)}, f32[4,128,128]{2,1,0:T(8,128)}, f32[4,128,128]{2,1,0:T(8,128)}) custom-call(bf16[16,256,128]{2,1,0:T(8,128)(2,1)S(1)} %get-tuple-element.9.refs_0_, f32[4,128,128]{2,1,0:T(8,128)S(1)} %get-tuple-element.10.refs_1_, f32[4,128,128]{2,1,0:T(8,128)S(1)} %get-tuple-element.11.refs_2_), custom_call_target="tpu_custom_call" | custom-call | tf_op jit(solution)/shard_map/store/pallas_call | solution.py:603
